TPU v7x, 512 devices: a whole 4x8x8 slice. The times are simulated.
512 devices in a mesh: dp: 32 (over z, x), cent: 16 (over y, core).
Axes of the slice: x: 4, y: 8, z: 8, core: 2. Of those that a mesh axis runs over, the one named last changes fastest.
Arguments:
- embeds: bfloat16 [262144, 768], P(('dp', 'cent')), may hold values from -6 to 6
- coarse_ids: int32 [262144], P(('dp', 'cent')), may hold values from 0 to 127, as said below
- fine_ids: int32 [262144], P(('dp', 'cent')), may hold values from 0 to 16383, as said below
- coarse_cents: float32 [128, 768], replicated, may hold values from -3 to 3
- fine_cents: bfloat16 [128, 128, 768], P('cent'), may hold values from -3 to 3
Outputs:
- new_fine: float32 [128, 128, 768], P('cent', 'dp')
- new_coarse: float32 [128, 768], replicated
- fine_gaps: float32 [262144], P(('dp', 'cent'))
Inputs may be any that keep to these rules, and one draw needn't show every extreme that they name: `coarse_ids`: the coarse cluster c is owned by index c // 8 of cent. The embeddings of one device (each aligned block of 512 rows) fall in exactly 8 coarse clusters, no two with the same owner; at most 128 embeddings of one device lie in one cluster, and on every device one cluster holds exactly 128. fine_ids[r] // 128 equals coarse_ids[r].
All inputs are finite; a program needn't handle non-finite values.
Results may differ from a plain program's by a relative error of at most 0.00035.
Values may be sent and summed in bfloat16 or wider, within the bound.
No kernel may reach another device: no remote copies, remote signals or barrier semaphores. Data moves between devices by JAX's collectives and lax.ppermute only.
A program may use at most 64 MiB of HBM per device.

v0:
```python
import jax
import jax.numpy as jnp
from jax import lax
from jax.sharding import PartitionSpec as P

COARSE = 128


def distances(rows, cents):
    dots = lax.dot_general(
        rows, cents, (((1,), (1,)), ((), ())), preferred_element_type=jnp.float32
    )
    row_sq = jnp.einsum("rd,rd->r", rows, rows, preferred_element_type=jnp.float32)
    cent_sq = jnp.einsum("fd,fd->f", cents, cents, preferred_element_type=jnp.float32)
    return (row_sq[:, None] - 2.0 * dots + cent_sq[None, :]) / rows.shape[1]


def column_sums(onehot, rows):
    return lax.dot_general(
        onehot, rows, (((0,), (0,)), ((), ())), preferred_element_type=jnp.float32
    )


def body(embeds, coarse_ids, fine_ids, coarse_cents, fine_cents):
    owners = lax.axis_size("cent")
    blk, per, width = fine_cents.shape
    rows = embeds.shape[0]
    me = lax.axis_index("cent")
    anchor_coarse = rows * lax.axis_size("dp") * owners // COARSE
    anchor_fine = max(1, anchor_coarse // per)
    coarse_hot = (coarse_ids[:, None] == jnp.arange(COARSE, dtype=jnp.int32)[None, :]).astype(
        jnp.bfloat16
    )
    coarse_part = column_sums(coarse_hot, embeds)
    coarse_count = jnp.sum(coarse_hot.astype(jnp.float32), axis=0)
    coarse_sum, coarse_num = lax.psum((coarse_part, coarse_count), ("dp", "cent"))
    new_coarse = (anchor_coarse * coarse_cents + coarse_sum) / (anchor_coarse + coarse_num[:, None])
    owner_row = coarse_ids // blk
    owner_ids = jnp.arange(owners, dtype=jnp.int32)
    owner_match = owner_row[:, None] == owner_ids[None, :]
    wanted = jnp.max(jnp.where(owner_match, coarse_ids[:, None], -1), axis=0)
    lists = lax.all_gather(wanted[None, :], "cent", axis=0, tiled=True)
    asked = lax.dynamic_index_in_dim(lists, me, 1, keepdims=False) - me * blk
    served = asked >= 0
    asked = jnp.where(served, asked, 0)
    assign = (
        (asked[None, :] == jnp.arange(blk, dtype=jnp.int32)[:, None]) & served[None, :]
    ).astype(jnp.float32)
    local = fine_ids - coarse_ids * per
    outgoing = jnp.where(served[:, None, None], fine_cents[asked], jnp.zeros((), jnp.bfloat16))
    arrived = lax.all_to_all(outgoing, "cent", split_axis=0, concat_axis=0, tiled=True)
    slots = owners // 2
    order = jnp.argsort(jnp.where(wanted >= 0, owner_ids, owners))[:slots]
    chosen = arrived[order].reshape(slots * per, width)
    slot_ids = jnp.arange(slots, dtype=jnp.int32)
    slot_row = jnp.sum(
        jnp.where(owner_row[:, None] == order[None, :], slot_ids[None, :], 0), axis=1
    )
    dist = distances(embeds, chosen)
    columns = jnp.arange(slots * per, dtype=jnp.int32)
    gaps = jnp.min(jnp.where((columns // per)[None, :] == slot_row[:, None], dist, jnp.inf), axis=1)
    fine_hot = (columns[None, :] == (slot_row * per + local)[:, None]).astype(jnp.bfloat16)
    part = column_sums(fine_hot, embeds).reshape(slots, per, width)
    count = jnp.sum(fine_hot.astype(jnp.float32), axis=0).reshape(slots, per)
    back_sum = jnp.zeros((owners, per, width), jnp.float32).at[order].set(part)
    back_count = jnp.zeros((owners, per), jnp.float32).at[order].set(count)
    home_sum, home_count = (
        lax.all_to_all(back_sum, "cent", split_axis=0, concat_axis=0, tiled=True),
        lax.all_to_all(back_count, "cent", split_axis=0, concat_axis=0, tiled=True),
    )
    block_sum = jnp.einsum("bp,pfd->bfd", assign, home_sum, precision=lax.Precision.HIGHEST)
    block_count = jnp.einsum("bp,pf->bf", assign, home_count, precision=lax.Precision.HIGHEST)
    fine_sum, fine_num = (
        lax.psum_scatter(block_sum, "dp", scatter_dimension=1, tiled=True),
        lax.psum_scatter(block_count, "dp", scatter_dimension=1, tiled=True),
    )
    share = per // lax.axis_size("dp")
    former = lax.dynamic_slice_in_dim(fine_cents, lax.axis_index("dp") * share, share, 1).astype(
        jnp.float32
    )
    new_fine = (anchor_fine * former + fine_sum) / (anchor_fine + fine_num[:, :, None])
    return (new_fine, new_coarse, gaps)


def solution(mesh):
    placed = (
        P(("dp", "cent"), None),
        P(("dp", "cent")),
        P(("dp", "cent")),
        P(),
        P("cent", None, None),
    )
    return jax.shard_map(
        body,
        mesh=mesh,
        in_specs=placed,
        out_specs=(P("cent", "dp", None), P(), P(("dp", "cent"))),
        check_vma=False,
    )
```

profile of v0, /device:TPU:32, one launch (start us, length us, event | category | flops | bytes accessed | tf_op | source)
XLA Modules:
  0.0 527.4 jit_solution(10182061954585838722)
XLA Ops:
  8.0 0.8 add_select_fusion.1
  8.8 0.8 select_reduce_fusion
  9.6 1.2 sort.17
  11.0 0.7 subtract_add_fusion
  11.7 0.3 convert_reduce_fusion
  12.0 1.2 scatter_custom_fusion.1
  13.1 8.8 %all-to-all-start.1 = ((f32[16,1,128]{2,1,0:T(1,128)}), f32[16,1,128]{2,1,0:T(1,128)S(1)}, u32[]{:S(2)}, u32[]{:S(2)}) async-start(f32[16,1,128]{2,1,0:T(1,128)} %bitcast.4), calls=%async_computation.2 | async-start | bytes 16384 | tf_op jit(solution)/shard_map/all_to_all | solution.py:69
  21.9 3.9 fusion.5
  25.8 3.3 broadcast_in_dim.83
  29.1 6.9 %scatter_fusion = f32[16,128,768]{2,1,0:T(8,128)} fusion(f32[16,128,768]{2,1,0:T(8,128)} %broadcast_in_dim.83, s32[8]{0:T(128)S(1)} %get-tuple-element.23, f32[8,128,768]{2,1,0:T(8,128)} %bitcast.23), kind=kCustom, calls=%fused_computation.2 | custom fusion | bytes 9437216 | tf_op jit(solution)/shard_map/scatter | solution.py:65
  36.0 7.4 %all-to-all-start = ((f32[16,128,768]{2,1,0:T(8,128)}), f32[16,128,768]{2,1,0:T(8,128)}, u32[]{:S(2)}, u32[]{:S(2)}) async-start(f32[16,128,768]{2,1,0:T(8,128)} %scatter_fusion), calls=%async_computation | async-start | bytes 12582912 | tf_op jit(solution)/shard_map/all_to_all | solution.py:68
  43.5 1.1 fusion.9
  44.6 1.3 dynamic-slice
  46.6 0.2 dynamic-update-slice
  46.9 142.0 %all-reduce.1 = s32[16,16]{1,0:T(8,128)S(1)} all-reduce(s32[16,16]{1,0:T(8,128)S(1)} %reshape.94), channel_id=2, replica_groups=mesh['dp'=32,'cent'=16] {'cent'}, use_global_device_ids=true, to_apply=%add | all-reduce | flops 256 | bytes 2048
  188.9 0.2 fusion.11
  189.1 2.4 gather_fusion
  191.5 3.8 broadcast_select_fusion
  195.4 7.2 %all-to-all-start.2 = ((bf16[16,128,768]{2,1,0:T(8,128)(2,1)}), bf16[16,128,768]{2,1,0:T(8,128)(2,1)}, u32[]{:S(2)}, u32[]{:S(2)}) async-start(bf16[16,128,768]{2,1,0:T(8,128)(2,1)} %broadcast_select_fusion), calls=%async_computation.3 | async-start | bytes 6291456 | tf_op jit(solution)/shard_map/all_to_all | solution.py:51
  202.6 10.0 %fusion = f32[8,128,768]{2,0,1:T(8,128)} fusion(f32[16,128,768]{2,1,0:T(8,128)} %all-to-all-done, s32[16]{0:T(128)S(1)} %broadcast_select_fusion.1, pred[16]{0:T(512)(128)(4,1)S(1)} %broadcast_compare_fusion), kind=kOutput, calls=%fused_computation.4 | convolution fusion | flops 150995200 | bytes 9437264 | tf_op jit(solution)/shard_map/bp,pfd->bfd/dot_general | solution.py:71
  212.7 1.3 dynamic-slice.1
  214.6 0.1 convert_reduce_fusion.1
  214.8 153.5 %psum.15 = f32[128]{0:T(128)S(1)} all-reduce(f32[128]{0:T(128)S(1)} %convert_reduce_fusion.1), channel_id=1, replica_groups=mesh['dp'=32,'cent'=16] {'dp','cent'}, use_global_device_ids=true, to_apply=%region_10.11 | all-reduce | flops 128 | bytes 1024 | tf_op jit(solution)/shard_map/psum | solution.py:36
  368.4 0.2 fusion.6
  368.6 0.3 fusion.19
  368.9 141.6 %all-reduce.2 = f32[8,128]{0,1:T(8,128)S(1)} all-reduce(f32[8,128]{0,1:T(8,128)S(1)} %fusion.19), channel_id=4, replica_groups=mesh['dp'=32,'cent'=16] {'dp'}, use_global_device_ids=true, to_apply=%region_7.8.clone | all-reduce | flops 1024 | bytes 8192
  510.6 1.8 add_divide_fusion
  512.4 2.5 gather_fusion.1
  515.0 0.4 fusion.2
  515.3 2.9 fusion.3
  518.3 1.0 add_divide_fusion.1
  519.3 0.7 copy.22
  (31 shorter events, 0.4 us)
Async XLA Ops:
  8.0 181.1 %copy-start = (bf16[8,128,768]{2,1,0:T(8,128)(2,1)S(1)}, bf16[8,128,768]{2,1,0:T(8,128)(2,1)}, u32[]{:S(2)}) copy-start(bf16[8,128,768]{2,1,0:T(8,128)(2,1)} %param.9) | copy-start | bytes 4718596
  13.1 22.9 %all-to-all-start.1 = ((f32[16,1,128]{2,1,0:T(1,128)}), f32[16,1,128]{2,1,0:T(1,128)S(1)}, u32[]{:S(2)}, u32[]{:S(2)}) async-start(f32[16,1,128]{2,1,0:T(1,128)} %bitcast.4), calls=%async_computation.2 | async-start | bytes 16384 | tf_op jit(solution)/shard_map/all_to_all | solution.py:69
  36.0 7.4 %copy-start.1 = (bf16[512,768]{1,0:T(8,128)(2,1)S(1)}, bf16[512,768]{1,0:T(8,128)(2,1)}, u32[]{:S(2)}) copy-start(bf16[512,768]{1,0:T(8,128)(2,1)} %param.5) | copy-start | bytes 2359300
  36.0 7.4 %copy-start.3 = (s32[512]{0:T(512)S(1)}, s32[512]{0:T(512)}, u32[]{:S(2)}) copy-start(s32[512]{0:T(512)} %param.6) | copy-start | bytes 6148
  36.0 159.3 %all-to-all-start = ((f32[16,128,768]{2,1,0:T(8,128)}), f32[16,128,768]{2,1,0:T(8,128)}, u32[]{:S(2)}, u32[]{:S(2)}) async-start(f32[16,128,768]{2,1,0:T(8,128)} %scatter_fusion), calls=%async_computation | async-start | bytes 12582912 | tf_op jit(solution)/shard_map/all_to_all | solution.py:68
  43.4 467.2 %all-reduce.5.cloned.1.call-start = ((), (), s32[]{:S(2)}) async-start(), calls=%async_computation.5 | async-start | bytes 786432 | tf_op jit(solution)/shard_map/psum | solution.py:36
  195.4 317.1 %all-to-all-start.2 = ((bf16[16,128,768]{2,1,0:T(8,128)(2,1)}), bf16[16,128,768]{2,1,0:T(8,128)(2,1)}, u32[]{:S(2)}, u32[]{:S(2)}) async-start(bf16[16,128,768]{2,1,0:T(8,128)(2,1)} %broadcast_select_fusion), calls=%async_computation.3 | async-start | bytes 6291456 | tf_op jit(solution)/shard_map/all_to_all | solution.py:51
  202.6 315.7 %reduce-scatter.2.cloned.1.call-start = ((), (), s32[]{:S(2)}) async-start(), calls=%async_computation.4 | async-start | bytes 3244032 | tf_op jit(solution)/shard_map/reduce_scatter | solution.py:74
  212.6 297.9 %copy-start.2 = (f32[128,768]{1,0:T(8,128)S(1)}, f32[128,768]{1,0:T(8,128)}, u32[]{:S(2)}) copy-start(f32[128,768]{1,0:T(8,128)} %param.8) | copy-start | bytes 1179652
Sparse Core Ops, SparseCore 0:
  50.6 357.0 all-reduce.4
Sparse Core Ops, SparseCore 1:
  212.8 228.6 reduce-scatter.1
where the time goes:
time: 528 us; the launch traced here: 527 us
  blocking collectives  437 us (83%)
  starting transfers between devices  23.5 us (4%)
  local copies, waits for them, and re-layouts  20 us (4%)
  matrix products  18.3 us (3%)
  between operations  16.9 us (3%)
  other arithmetic  11.6 us (2%)
    unnamed x2, blocking collectives  284 us
    psum x1, blocking collectives, body(): lax.psum((coarse_part, coarse_count), ('dp', 'cent'))  154 us
  transfers between devices with their start and end apart: 5, of which 0 were waited for; matrix products, arithmetic and copies ran while one was open for 8% of the time, Pallas kernels for 0%

commit v1 on v0

v1 whole, which is shorter than its diff:
```python
import functools

import jax
import jax.numpy as jnp
from jax import lax
from jax.experimental import pallas as pl
from jax.experimental.pallas import tpu as pltpu
from jax.sharding import Mesh, PartitionSpec as P

COARSE = 128
DP = ("z", "x")
CENT = ("y", "core")
PARTS = 3


def sums_kernel(pick, key_ref, target_ref, rows_ref, out_ref):
    source = pl.program_id(0)

    @pl.when(source == 0)
    def _():
        out_ref[...] = jnp.zeros_like(out_ref)

    hot = (target_ref[...] == key_ref[0]).astype(jnp.bfloat16)
    part = jnp.dot(hot, rows_ref[0], preferred_element_type=jnp.float32)
    pair = pick[source] // 2
    out_ref[:, pair] += part.reshape(out_ref.shape[0], 8, part.shape[1])


def fine_sums(pick, keys, target, rows, per_source):
    sources, _, width = rows.shape
    groups = target.shape[0] // 8
    pairs = 4
    return pl.pallas_call(
        sums_kernel,
        grid_spec=pltpu.PrefetchScalarGridSpec(
            num_scalar_prefetch=1,
            grid=(sources,),
            in_specs=[
                pl.BlockSpec((1, 1, per_source), lambda s, pick: (s, 0, 0)),
                pl.BlockSpec((groups * 8, 1), lambda s, pick: (0, 0)),
                pl.BlockSpec((1, per_source, width), lambda s, pick: (s, 0, 0)),
            ],
            out_specs=pl.BlockSpec((groups, pairs, 8, width), lambda s, pick: (0, 0, 0, 0)),
        ),
        out_shape=jax.ShapeDtypeStruct((groups, pairs, 8, width), jnp.float32),
        compiler_params=pltpu.CompilerParams(vmem_limit_bytes=32 * 2**20),
    )(pick, keys, target, rows)


def gaps_kernel(pick, cents_ref, square_ref, *refs):
    out_ref = refs[-1]
    dots = None
    start = 0
    for rows_ref in refs[:-1]:
        width = rows_ref.shape[2]
        term = lax.dot_general(
            cents_ref[0, :, start : start + width],
            rows_ref[0],
            (((1,), (1,)), ((), ())),
            preferred_element_type=jnp.float32,
        )
        dots = term if dots is None else dots + term
        start += width
    out_ref[0] = jnp.min(square_ref[0] - 2.0 * dots, axis=0, keepdims=True)


def nearest(pick, cents, squares, rows, per_source):
    sources = rows[0].shape[0]
    per, width = cents.shape[1:]
    return pl.pallas_call(
        gaps_kernel,
        grid_spec=pltpu.PrefetchScalarGridSpec(
            num_scalar_prefetch=1,
            grid=(sources,),
            in_specs=[
                pl.BlockSpec((1, per, width), lambda s, pick: (pick[s], 0, 0)),
                pl.BlockSpec((1, per, 1), lambda s, pick: (pick[s], 0, 0)),
            ]
            + [pl.BlockSpec((1, per_source, r.shape[2]), lambda s, pick: (s, 0, 0)) for r in rows],
            out_specs=pl.BlockSpec((1, 1, per_source), lambda s, pick: (s, 0, 0)),
        ),
        out_shape=jax.ShapeDtypeStruct((sources, 1, per_source), jnp.float32),
        compiler_params=pltpu.CompilerParams(vmem_limit_bytes=32 * 2**20),
    )(pick, cents, squares, *rows)


def body(embeds, coarse_ids, fine_ids, coarse_cents, fine_cents):
    blk, per, width = fine_cents.shape
    count = embeds.shape[0]
    depth, across = lax.axis_size("z"), lax.axis_size("x")
    planes = depth * across
    owners = lax.axis_size(CENT)
    share = per // planes
    me = lax.axis_index(CENT)
    anchor_coarse = count * planes * owners // COARSE
    anchor_fine = max(1, anchor_coarse // per)
    local = fine_ids - coarse_ids * per
    piece = width // PARTS

    ids = jnp.concatenate([coarse_ids, local]).astype(jnp.bfloat16).reshape(-1, piece)
    ids = jnp.pad(ids, ((0, 16 - ids.shape[0]), (0, 0)))
    gathered = []
    for k in range(PARTS):
        block = embeds[:, k * piece : (k + 1) * piece]
        if k == 0:
            block = jnp.concatenate([block, ids], axis=0)
        gathered.append(lax.all_gather(block, CENT, axis=0, tiled=False))

    coarse_hot = (jnp.arange(COARSE, dtype=jnp.int32)[:, None] == coarse_ids[None, :]).astype(jnp.bfloat16)
    fine_hot = (local[:, None] == jnp.arange(per, dtype=jnp.int32)[None, :]).astype(jnp.bfloat16)
    coarse_part = jnp.dot(
        coarse_hot, jnp.concatenate([embeds, fine_hot], axis=1), preferred_element_type=jnp.float32
    )
    coarse_part = coarse_part.reshape(planes, COARSE // planes, width + per)
    mine = jnp.sum(lax.all_to_all(coarse_part, DP, split_axis=0, concat_axis=0, tiled=True), axis=0)
    mine = jnp.sum(lax.all_gather(mine, CENT, axis=0, tiled=False), axis=0)
    totals = lax.all_to_all(
        jnp.broadcast_to(mine[None], (planes,) + mine.shape), DP, split_axis=0, concat_axis=0, tiled=True
    ).reshape(COARSE, width + per)
    counts = totals[:, width:]
    new_coarse = (anchor_coarse * coarse_cents + totals[:, :width]) / (
        anchor_coarse + jnp.sum(counts, axis=1, keepdims=True)
    )

    sent = gathered[0][:, count : count + 2 * count // piece, :].reshape(owners, 2, count).astype(jnp.int32)
    cluster = sent[:, 0] - me * blk
    ours = (cluster >= 0) & (cluster < blk)
    pick = jnp.max(jnp.where(ours, cluster, 0), axis=1)
    keys = jnp.where(ours, (cluster % 2) * per + sent[:, 1], -1)[:, None, :]
    slot = jnp.arange(2 * per, dtype=jnp.int32)
    group, half, inner = slot // (2 * share), (slot // share) % 2, slot % share
    target = (half * per + (group % depth) * across * share + (group // depth) * share + inner)[:, None]

    fine_parts = []
    for k in range(PARTS):
        part = fine_sums(pick, keys, target, gathered[k], count).reshape(across, depth, blk * share, piece)
        part = jnp.sum(lax.all_to_all(part, "x", split_axis=0, concat_axis=0, tiled=True), axis=0)
        part = jnp.sum(lax.all_to_all(part, "z", split_axis=0, concat_axis=0, tiled=True), axis=0)
        fine_parts.append(part.reshape(blk, share, piece))
    fine_sum = jnp.concatenate(fine_parts, axis=2)
    first = lax.axis_index(DP) * share
    former = lax.dynamic_slice_in_dim(fine_cents, first, share, 1).astype(jnp.float32)
    fine_num = lax.dynamic_slice(counts, (me * blk, first), (blk, share))
    new_fine = (anchor_fine * former + fine_sum) / (anchor_fine + fine_num[:, :, None])

    squares = jnp.sum(jnp.square(fine_cents.astype(jnp.float32)), axis=2, keepdims=True)
    least = nearest(pick, fine_cents, squares, gathered, count)
    back = lax.all_to_all(least, CENT, split_axis=0, concat_axis=0, tiled=True)[:, 0]
    row_sq = jnp.sum(jnp.square(embeds.astype(jnp.float32)), axis=1)
    at = (coarse_ids // blk)[None, :] == jnp.arange(owners, dtype=jnp.int32)[:, None]
    gaps = (row_sq + jnp.sum(jnp.where(at, back, 0.0), axis=0)) / width
    return (new_fine, new_coarse, gaps)


def solution(mesh):
    fine_mesh = Mesh(mesh.devices.reshape(8, 4, 8, 2), DP + CENT)
    placed = (P(DP + CENT, None), P(DP + CENT), P(DP + CENT), P(), P(CENT, None, None))
    return jax.shard_map(
        body,
        mesh=fine_mesh,
        in_specs=placed,
        out_specs=(P(CENT, DP, None), P(), P(DP + CENT)),
        check_vma=False,
    )
```

time: 528 us -> 292 us (0.55)
  the two profiles are of different devices: /device:TPU:32 before, /device:TPU:8 now
where the time goes in v1:
time: 292 us; the launch traced here: 290 us
  waiting for transfers between devices  133 us (46%)
  blocking collectives  46.6 us (16%)
  starting transfers between devices  36.7 us (13%)
  Pallas kernels  27.4 us (9%)
  local copies, waits for them, and re-layouts  17.8 us (6%)
  other arithmetic  14.1 us (5%)
  between operations  14 us (5%)
    all_gather x3, waiting for transfers between devices, body(): gathered.append(lax.all_gather(block, CENT, axis=0, tiled=False))  85.1 us
    all_to_all x1, blocking collectives, body(): lax.all_to_all(coarse_part, DP, split_axis=0, concat_axis=0, tiled=True)  29.7 us
    all_to_all x3, waiting for transfers between devices, body(): lax.all_to_all(part, 'x', split_axis=0, concat_axis=0, tiled=True)  24.7 us
    all_to_all x3, waiting for transfers between devices, body(): lax.all_to_all(part, 'z', split_axis=0, concat_axis=0, tiled=True)  22.3 us
    pallas_call x3, Pallas kernels, fine_sums(): pl.pallas_call(sums_kernel, grid_spec=pltpu.PrefetchScalarGridSpec(num_sc...  18.6 us
    all_gather x1, blocking collectives, body(): mine = jnp.sum(lax.all_gather(mine, CENT, axis=0, tiled=False), axis=0)  17 us
    all_to_all x3, starting transfers between devices, body(): lax.all_to_all(part, 'z', split_axis=0, concat_axis=0, tiled=True)  14.8 us
    unnamed x26, local copies, waits for them, and re-layouts  13.2 us
  transfers between devices with their start and end apart: 11, of which 8 were waited for; matrix products, arithmetic and copies ran while one was open for 5% of the time, Pallas kernels for 9%

profile of v1, /device:TPU:8, one launch (start us, length us, event | category | flops | bytes accessed | tf_op | source)
XLA Modules:
  0.0 290.4 jit_solution(1301541568267258703)
XLA Ops:
  8.1 2.0 fusion.44
  12.9 29.7 %all_to_all.45 = f32[32,4,896]{2,1,0:T(4,128)S(1)} all-to-all(f32[32,4,896]{2,1,0:T(4,128)S(1)} %reshape.244), channel_id=1, replica_groups=mesh['z'=8,'x'=4,'y'=8,'core'=2] {'z','x'}, dimensions={0} | all-to-all | bytes 917504 | tf_op jit(solution)/shard_map/all_to_all | solution.py:115
  42.7 17.0 %all-gather.4 = f32[16,4,896]{2,1,0:T(4,128)S(1)} all-gather(f32[1,4,896]{2,1,0:T(4,128)S(1)} %bitcast.31), channel_id=5, replica_groups=mesh['z'=8,'x'=4,'y'=8,'core'=2] {'y','core'}, dimensions={0}, use_global_device_ids=true | all-gather | bytes 243712 | tf_op jit(solution)/shard_map/all_gather | solution.py:116
  60.6 4.4 %all-to-all-start.7 = ((f32[32,4,896]{2,1,0:T(4,128)}), f32[32,4,896]{2,1,0:T(4,128)S(1)}, u32[]{:S(2)}, u32[]{:S(2)}) async-start(f32[32,4,896]{2,1,0:T(4,128)} %broadcast_in_dim.13), calls=%async_computation.7 | async-start | bytes 917504 | tf_op jit(solution)/shard_map/all_to_all | solution.py:117
  66.9 39.2 %all-gather.11.cloned.1.call-done = bf16[8192,256]{1,0:T(8,128)(2,1)} async-done(((bf16[512,256]{1,0:T(8,128)(2,1)}), bf16[8192,256]{1,0:T(8,128)(2,1)}) %all-gather.11.cloned.1.call-update) | async-done | bytes 4194320 | tf_op jit(solution)/shard_map/all_gather | solution.py:107
  106.0 45.9 %all-gather.13.cloned.1.call-done = bf16[8192,256]{1,0:T(8,128)(2,1)} async-done(((bf16[512,256]{1,0:T(8,128)(2,1)}), bf16[8192,256]{1,0:T(8,128)(2,1)}) %all-gather.13.cloned.1.call-update) | async-done | bytes 4194320 | tf_op jit(solution)/shard_map/all_gather | solution.py:107
  151.9 2.2 copy-done
  154.2 2.2 copy-done.2
  156.4 2.2 copy-done.4
  158.5 8.9 %shard_map.79 = f32[16,1,512]{2,1,0:T(1,128)} custom-call(s32[16]{0:T(128)S(1)} %fusion.35.pick, bf16[8,128,768]{2,1,0:T(8,128)(2,1)S(1)} %copy-done.6, f32[8,128,1]{2,1,0:T(8,128)S(1)} %copy.10.square_ref, bf16[16,528,256]{2,1,0:T(8,128)(2,1)S(1)} %bitcast.25, bf16[16,512,256]{2,1,0:T(8,128)(2,1)S(1)} %bitcast.27, bf16[16,512,256]{2,1,0:T(8,128)(2,1)S(1)} %bitcast.29), custom_call_target="tpu_custom_call" | custom-call | tf_op jit(solution)/shard_map/pallas_call | solution.py:70
  167.4 5.3 %all-to-all-start.8 = ((f32[16,1,512]{2,1,0:T(1,128)}), f32[16,1,512]{2,1,0:T(1,128)S(1)}, u32[]{:S(2)}, u32[]{:S(2)}) async-start(f32[16,1,512]{2,1,0:T(1,128)} %shard_map.79), calls=%async_computation.8 | async-start | bytes 65536 | tf_op jit(solution)/shard_map/all_to_all | solution.py:148
  172.8 2.2 copy-done.1
  175.1 6.2 %shard_map.76 = f32[32,4,8,256]{3,2,1,0:T(8,128)} custom-call(s32[16]{0:T(128)S(1)} %fusion.35.pick, s32[16,1,512]{2,1,0:T(1,128)S(1)} %get-tuple-element.3.key_ref, s32[256,1]{1,0:T(8,128)S(1)} %fusion.16.target_ref, bf16[16,528,256]{2,1,0:T(8,128)(2,1)S(1)} %bitcast.26), custom_call_target="tpu_custom_call" | custom-call | tf_op jit(solution)/shard_map/pallas_call | solution.py:33
  181.2 4.2 %all-to-all-start = ((f32[4,8,32,256]{3,2,1,0:T(8,128)}), f32[4,8,32,256]{3,2,1,0:T(8,128)S(1)}, u32[]{:S(2)}, u32[]{:S(2)}) async-start(f32[4,8,32,256]{3,2,1,0:T(8,128)} %bitcast.1), calls=%async_computation | async-start | bytes 2097152 | tf_op jit(solution)/shard_map/all_to_all | solution.py:137
  185.5 2.2 copy-done.5
  187.7 6.2 %shard_map.78 = f32[32,4,8,256]{3,2,1,0:T(8,128)} custom-call(s32[16]{0:T(128)S(1)} %fusion.35.pick, s32[16,1,512]{2,1,0:T(1,128)S(1)} %get-tuple-element.3.key_ref, s32[256,1]{1,0:T(8,128)S(1)} %fusion.16.target_ref, bf16[16,512,256]{2,1,0:T(8,128)(2,1)S(1)} %bitcast.30), custom_call_target="tpu_custom_call" | custom-call | tf_op jit(solution)/shard_map/pallas_call | solution.py:33
  193.9 7.0 %all-to-all-done = f32[4,8,32,256]{3,2,1,0:T(8,128)S(1)} async-done(((f32[4,8,32,256]{3,2,1,0:T(8,128)}), f32[4,8,32,256]{3,2,1,0:T(8,128)S(1)}, u32[]{:S(2)}, u32[]{:S(2)}) %all-to-all-start) | async-done | bytes 1048608 | tf_op jit(solution)/shard_map/all_to_all | solution.py:137
  200.9 4.2 %all-to-all-start.4 = ((f32[4,8,32,256]{3,2,1,0:T(8,128)}), f32[4,8,32,256]{3,2,1,0:T(8,128)}, u32[]{:S(2)}, u32[]{:S(2)}) async-start(f32[4,8,32,256]{3,2,1,0:T(8,128)} %bitcast.5), calls=%async_computation.4 | async-start | bytes 2097152 | tf_op jit(solution)/shard_map/all_to_all | solution.py:137
  205.1 2.2 copy-done.3
  207.3 6.2 %shard_map.77 = f32[32,4,8,256]{3,2,1,0:T(8,128)} custom-call(s32[16]{0:T(128)S(1)} %fusion.35.pick, s32[16,1,512]{2,1,0:T(1,128)S(1)} %get-tuple-element.3.key_ref, s32[256,1]{1,0:T(8,128)S(1)} %fusion.16.target_ref, bf16[16,512,256]{2,1,0:T(8,128)(2,1)S(1)} %bitcast.28), custom_call_target="tpu_custom_call" | custom-call | tf_op jit(solution)/shard_map/pallas_call | solution.py:33
  213.5 6.2 %all-to-all-done.4 = f32[4,8,32,256]{3,2,1,0:T(8,128)} async-done(((f32[4,8,32,256]{3,2,1,0:T(8,128)}), f32[4,8,32,256]{3,2,1,0:T(8,128)}, u32[]{:S(2)}, u32[]{:S(2)}) %all-to-all-start.4) | async-done | bytes 1048608 | tf_op jit(solution)/shard_map/all_to_all | solution.py:137
  219.7 3.5 %all-to-all-start.2 = ((f32[4,8,32,256]{3,2,1,0:T(8,128)}), f32[4,8,32,256]{3,2,1,0:T(8,128)S(1)}, u32[]{:S(2)}, u32[]{:S(2)}) async-start(f32[4,8,32,256]{3,2,1,0:T(8,128)} %bitcast.3), calls=%async_computation.2 | async-start | bytes 2097152 | tf_op jit(solution)/shard_map/all_to_all | solution.py:137
  223.3 2.1 reduce_sum.108
  225.4 11.5 %all-to-all-done.2 = f32[4,8,32,256]{3,2,1,0:T(8,128)S(1)} async-done(((f32[4,8,32,256]{3,2,1,0:T(8,128)}), f32[4,8,32,256]{3,2,1,0:T(8,128)S(1)}, u32[]{:S(2)}, u32[]{:S(2)}) %all-to-all-start.2) | async-done | bytes 1048608 | tf_op jit(solution)/shard_map/all_to_all | solution.py:137
  236.8 7.4 %all-to-all-start.1 = ((f32[8,32,256]{2,1,0:T(8,128)}), f32[8,32,256]{2,1,0:T(8,128)}, u32[]{:S(2)}, u32[]{:S(2)}) async-start(f32[8,32,256]{2,1,0:T(8,128)} %reduce_sum.108), calls=%async_computation.1 | async-start | bytes 524288 | tf_op jit(solution)/shard_map/all_to_all | solution.py:138
  244.2 2.0 reduce_sum.112
  246.2 8.6 %all-to-all-done.1 = f32[8,32,256]{2,1,0:T(8,128)} async-done(((f32[8,32,256]{2,1,0:T(8,128)}), f32[8,32,256]{2,1,0:T(8,128)}, u32[]{:S(2)}, u32[]{:S(2)}) %all-to-all-start.1) | async-done | bytes 262176 | tf_op jit(solution)/shard_map/all_to_all | solution.py:138
  254.8 4.0 %all-to-all-start.5 = ((f32[8,32,256]{2,1,0:T(8,128)}), f32[8,32,256]{2,1,0:T(8,128)}, u32[]{:S(2)}, u32[]{:S(2)}) async-start(f32[8,32,256]{2,1,0:T(8,128)} %reduce_sum.112), calls=%async_computation.5 | async-start | bytes 524288 | tf_op jit(solution)/shard_map/all_to_all | solution.py:138
  259.1 1.2 reshape.245
  261.8 7.6 %all-to-all-done.5 = f32[8,32,256]{2,1,0:T(8,128)} async-done(((f32[8,32,256]{2,1,0:T(8,128)}), f32[8,32,256]{2,1,0:T(8,128)}, u32[]{:S(2)}, u32[]{:S(2)}) %all-to-all-start.5) | async-done | bytes 262176 | tf_op jit(solution)/shard_map/all_to_all | solution.py:138
  269.3 3.4 %all-to-all-start.3 = ((f32[8,32,256]{2,1,0:T(8,128)}), f32[8,32,256]{2,1,0:T(8,128)S(1)}, u32[]{:S(2)}, u32[]{:S(2)}) async-start(f32[8,32,256]{2,1,0:T(8,128)} %reduce_sum.110), calls=%async_computation.3 | async-start | bytes 524288 | tf_op jit(solution)/shard_map/all_to_all | solution.py:138
  277.0 6.2 %all-to-all-done.3 = f32[8,32,256]{2,1,0:T(8,128)S(1)} async-done(((f32[8,32,256]{2,1,0:T(8,128)}), f32[8,32,256]{2,1,0:T(8,128)S(1)}, u32[]{:S(2)}, u32[]{:S(2)}) %all-to-all-start.3) | async-done | bytes 262176 | tf_op jit(solution)/shard_map/all_to_all | solution.py:138
  (62 shorter events, 13.2 us)
Async XLA Ops:
  7.2 5.3 %copy-start.12 = (s32[512]{0:T(512)S(1)}, s32[512]{0:T(512)}, u32[]{:S(2)}) copy-start(s32[512]{0:T(512)} %param.6) | copy-start | bytes 6148
  7.2 5.3 %copy-start.8 = (bf16[512,768]{1,0:T(8,128)(2,1)S(1)}, bf16[512,768]{1,0:T(8,128)(2,1)}, u32[]{:S(2)}) copy-start(bf16[512,768]{1,0:T(8,128)(2,1)} %param.5) | copy-start | bytes 2359300
  7.2 58.4 %all-gather.9.cloned.1.call-start = ((), (), s32[]{:S(2)}) async-start(), calls=%async_computation.9 | async-start | bytes 4595712 | tf_op jit(solution)/shard_map/all_gather | solution.py:107
  10.8 95.2 %all-gather.11.cloned.1.call-start = ((), (), s32[]{:S(2)}) async-start(), calls=%async_computation.10 | async-start | bytes 4456448 | tf_op jit(solution)/shard_map/all_gather | solution.py:107
  11.6 140.4 %all-gather.13.cloned.1.call-start = ((), (), s32[]{:S(2)}) async-start(), calls=%async_computation.11 | async-start | bytes 4456448 | tf_op jit(solution)/shard_map/all_gather | solution.py:107
  12.9 52.1 %copy-start.6 = (bf16[8,128,768]{2,1,0:T(8,128)(2,1)S(1)}, bf16[8,128,768]{2,1,0:T(8,128)(2,1)}, u32[]{:S(2)}) copy-start(bf16[8,128,768]{2,1,0:T(8,128)(2,1)} %cents_ref.1) | copy-start | bytes 4718596
  60.6 106.8 %all-to-all-start.7 = ((f32[32,4,896]{2,1,0:T(4,128)}), f32[32,4,896]{2,1,0:T(4,128)S(1)}, u32[]{:S(2)}, u32[]{:S(2)}) async-start(f32[32,4,896]{2,1,0:T(4,128)} %broadcast_in_dim.13), calls=%async_computation.7 | async-start | bytes 917504 | tf_op jit(solution)/shard_map/all_to_all | solution.py:117
  151.9 2.2 copy-start
  154.2 2.2 copy-start.2
  156.4 2.2 copy-start.4
  167.4 13.8 %copy-start.10 = (f32[32,4,896]{2,1,0:T(4,128)}, f32[32,4,896]{2,1,0:T(4,128)S(1)}, u32[]{:S(2)}) copy-start(f32[32,4,896]{2,1,0:T(4,128)S(1)} %all-to-all-done.7) | copy-start | bytes 1376260
  167.4 13.8 %all-to-all-start.8 = ((f32[16,1,512]{2,1,0:T(1,128)}), f32[16,1,512]{2,1,0:T(1,128)S(1)}, u32[]{:S(2)}, u32[]{:S(2)}) async-start(f32[16,1,512]{2,1,0:T(1,128)} %shard_map.79), calls=%async_computation.8 | async-start | bytes 65536 | tf_op jit(solution)/shard_map/all_to_all | solution.py:148
  172.8 2.2 copy-start.1
  181.2 19.7 %all-to-all-start = ((f32[4,8,32,256]{3,2,1,0:T(8,128)}), f32[4,8,32,256]{3,2,1,0:T(8,128)S(1)}, u32[]{:S(2)}, u32[]{:S(2)}) async-start(f32[4,8,32,256]{3,2,1,0:T(8,128)} %bitcast.1), calls=%async_computation | async-start | bytes 2097152 | tf_op jit(solution)/shard_map/all_to_all | solution.py:137
  185.5 2.2 copy-start.5
  200.9 12.6 %copy-start.7 = (f32[4,8,32,256]{3,2,1,0:T(8,128)}, f32[4,8,32,256]{3,2,1,0:T(8,128)S(1)}, u32[]{:S(2)}) copy-start(f32[4,8,32,256]{3,2,1,0:T(8,128)S(1)} %all-to-all-done) | copy-start | bytes 3145732
  200.9 18.8 %all-to-all-start.4 = ((f32[4,8,32,256]{3,2,1,0:T(8,128)}), f32[4,8,32,256]{3,2,1,0:T(8,128)}, u32[]{:S(2)}, u32[]{:S(2)}) async-start(f32[4,8,32,256]{3,2,1,0:T(8,128)} %bitcast.5), calls=%async_computation.4 | async-start | bytes 2097152 | tf_op jit(solution)/shard_map/all_to_all | solution.py:137
  205.1 2.2 copy-start.3
  219.7 17.1 %all-to-all-start.2 = ((f32[4,8,32,256]{3,2,1,0:T(8,128)}), f32[4,8,32,256]{3,2,1,0:T(8,128)S(1)}, u32[]{:S(2)}, u32[]{:S(2)}) async-start(f32[4,8,32,256]{3,2,1,0:T(8,128)} %bitcast.3), calls=%async_computation.2 | async-start | bytes 2097152 | tf_op jit(solution)/shard_map/all_to_all | solution.py:137
  223.3 35.6 %copy-start.9 = (bf16[512,768]{1,0:T(8,128)(2,1)S(1)}, bf16[512,768]{1,0:T(8,128)(2,1)}, u32[]{:S(2)}) copy-start(bf16[512,768]{1,0:T(8,128)(2,1)} %param.5) | copy-start | bytes 2359300
  236.8 18.0 %all-to-all-start.1 = ((f32[8,32,256]{2,1,0:T(8,128)}), f32[8,32,256]{2,1,0:T(8,128)}, u32[]{:S(2)}, u32[]{:S(2)}) async-start(f32[8,32,256]{2,1,0:T(8,128)} %reduce_sum.108), calls=%async_computation.1 | async-start | bytes 524288 | tf_op jit(solution)/shard_map/all_to_all | solution.py:138
  254.8 14.5 %all-to-all-start.5 = ((f32[8,32,256]{2,1,0:T(8,128)}), f32[8,32,256]{2,1,0:T(8,128)}, u32[]{:S(2)}, u32[]{:S(2)}) async-start(f32[8,32,256]{2,1,0:T(8,128)} %reduce_sum.112), calls=%async_computation.5 | async-start | bytes 524288 | tf_op jit(solution)/shard_map/all_to_all | solution.py:138
  259.1 13.7 %copy-start.11 = (f32[128,768]{1,0:T(8,128)S(1)}, f32[128,768]{1,0:T(8,128)}, u32[]{:S(2)}) copy-start(f32[128,768]{1,0:T(8,128)} %param.8) | copy-start | bytes 1179652
  269.3 13.8 %all-to-all-start.3 = ((f32[8,32,256]{2,1,0:T(8,128)}), f32[8,32,256]{2,1,0:T(8,128)S(1)}, u32[]{:S(2)}, u32[]{:S(2)}) async-start(f32[8,32,256]{2,1,0:T(8,128)} %reduce_sum.110), calls=%async_computation.3 | async-start | bytes 524288 | tf_op jit(solution)/shard_map/all_to_all | solution.py:138
Sparse Core Ops, SparseCore 0:
  10.9 49.2 all-gather.8
  62.4 43.6 all-gather.10
  108.2 43.7 all-gather.12

commit v2 on v1

v2 whole, which is shorter than its diff:
```python
import jax
import jax.numpy as jnp
from jax import lax
from jax.experimental import pallas as pl
from jax.experimental.pallas import tpu as pltpu
from jax.sharding import Mesh, PartitionSpec as P

COARSE = 128
DP = ("z", "x")
CENT = ("y", "core")
VMEM = 56 * 2**20


def sums_kernel(pick, key_ref, target_ref, rows_ref, out_ref):
    source = pl.program_id(0)

    @pl.when(source == 0)
    def _():
        out_ref[...] = jnp.zeros_like(out_ref)

    hot = (target_ref[...] == key_ref[0]).astype(jnp.bfloat16)
    part = jnp.dot(hot, rows_ref[0], preferred_element_type=jnp.float32)
    pair = pick[source] // 2
    out_ref[:, pair] += part.reshape(out_ref.shape[0], 8, part.shape[1])


def fine_sums(pick, keys, target, rows):
    sources, per_source, width = rows.shape
    groups = target.shape[0] // 8
    shape = (groups, 4, 8, width)
    return pl.pallas_call(
        sums_kernel,
        grid_spec=pltpu.PrefetchScalarGridSpec(
            num_scalar_prefetch=1,
            grid=(sources,),
            in_specs=[
                pl.BlockSpec((1, 1, per_source), lambda s, pick: (s, 0, 0)),
                pl.BlockSpec((groups * 8, 1), lambda s, pick: (0, 0)),
                pl.BlockSpec((1, per_source, width), lambda s, pick: (s, 0, 0)),
            ],
            out_specs=pl.BlockSpec(shape, lambda s, pick: (0, 0, 0, 0)),
        ),
        out_shape=jax.ShapeDtypeStruct(shape, jnp.float32),
        compiler_params=pltpu.CompilerParams(vmem_limit_bytes=VMEM),
        cost_estimate=pl.CostEstimate(
            flops=4 * groups * 4 * rows.size, bytes_accessed=2 * rows.size, transcendentals=0
        ),
    )(pick, keys, target, rows)


def gaps_kernel(pick, cents_ref, square_ref, rows_ref, out_ref):
    dots = lax.dot_general(
        cents_ref[0], rows_ref[0], (((1,), (1,)), ((), ())), preferred_element_type=jnp.float32
    )
    out_ref[0] = jnp.min(square_ref[0] - 2.0 * dots, axis=0, keepdims=True)


def nearest(pick, cents, squares, rows):
    sources, per_source, width = rows.shape
    per = cents.shape[1]
    return pl.pallas_call(
        gaps_kernel,
        grid_spec=pltpu.PrefetchScalarGridSpec(
            num_scalar_prefetch=1,
            grid=(sources,),
            in_specs=[
                pl.BlockSpec((1, per, width), lambda s, pick: (pick[s], 0, 0)),
                pl.BlockSpec((1, per, 1), lambda s, pick: (pick[s], 0, 0)),
                pl.BlockSpec((1, per_source, width), lambda s, pick: (s, 0, 0)),
            ],
            out_specs=pl.BlockSpec((1, 1, per_source), lambda s, pick: (s, 0, 0)),
        ),
        out_shape=jax.ShapeDtypeStruct((sources, 1, per_source), jnp.float32),
        compiler_params=pltpu.CompilerParams(vmem_limit_bytes=VMEM),
        cost_estimate=pl.CostEstimate(
            flops=2 * per * rows.size, bytes_accessed=2 * rows.size, transcendentals=0
        ),
    )(pick, cents, squares, rows)


def body(embeds, coarse_ids, fine_ids, coarse_cents, fine_cents):
    blk, per, width = fine_cents.shape
    count = embeds.shape[0]
    depth, across = lax.axis_size("z"), lax.axis_size("x")
    planes = depth * across
    owners = lax.axis_size(CENT)
    share = per // planes
    me = lax.axis_index(CENT)
    anchor_coarse = count * planes * owners // COARSE
    anchor_fine = max(1, anchor_coarse // per)
    local = fine_ids - coarse_ids * per

    rows = lax.all_gather(embeds, CENT, axis=0, tiled=False)
    sent = lax.all_gather(fine_ids, CENT, axis=0, tiled=False)

    coarse_hot = (jnp.arange(COARSE, dtype=jnp.int32)[:, None] == coarse_ids[None, :]).astype(jnp.bfloat16)
    fine_hot = (local[:, None] == jnp.arange(per, dtype=jnp.int32)[None, :]).astype(jnp.bfloat16)
    coarse_part = jnp.dot(
        coarse_hot, jnp.concatenate([embeds, fine_hot], axis=1), preferred_element_type=jnp.float32
    )
    coarse_part = coarse_part.reshape(planes, COARSE // planes, width + per)
    mine = jnp.sum(lax.all_to_all(coarse_part, DP, split_axis=0, concat_axis=0, tiled=True), axis=0)
    mine = jnp.sum(lax.all_gather(mine, CENT, axis=0, tiled=False), axis=0)
    totals = lax.all_to_all(
        jnp.broadcast_to(mine[None], (planes,) + mine.shape), DP, split_axis=0, concat_axis=0, tiled=True
    ).reshape(COARSE, width + per)
    counts = totals[:, width:]
    new_coarse = (anchor_coarse * coarse_cents + totals[:, :width]) / (
        anchor_coarse + jnp.sum(counts, axis=1, keepdims=True)
    )

    cluster = sent // per - me * blk
    ours = (cluster >= 0) & (cluster < blk)
    pick = jnp.max(jnp.where(ours, cluster, 0), axis=1)
    keys = jnp.where(ours, sent % (2 * per), -1)[:, None, :]
    slot = jnp.arange(2 * per, dtype=jnp.int32)
    group, half, inner = slot // (2 * share), (slot // share) % 2, slot % share
    target = (half * per + (group % depth) * across * share + (group // depth) * share + inner)[:, None]

    part = fine_sums(pick, keys, target, rows).reshape(across, depth, blk * share, width)
    part = jnp.sum(lax.all_to_all(part, "x", split_axis=0, concat_axis=0, tiled=True), axis=0)
    part = jnp.sum(lax.all_to_all(part, "z", split_axis=0, concat_axis=0, tiled=True), axis=0)
    fine_sum = part.reshape(blk, share, width)
    first = lax.axis_index(DP) * share
    former = lax.dynamic_slice_in_dim(fine_cents, first, share, 1).astype(jnp.float32)
    fine_num = lax.dynamic_slice(counts, (me * blk, first), (blk, share))
    new_fine = (anchor_fine * former + fine_sum) / (anchor_fine + fine_num[:, :, None])

    squares = jnp.sum(jnp.square(fine_cents.astype(jnp.float32)), axis=2, keepdims=True)
    least = nearest(pick, fine_cents, squares, rows)
    back = lax.all_to_all(least, CENT, split_axis=0, concat_axis=0, tiled=True)[:, 0]
    row_sq = jnp.sum(jnp.square(embeds.astype(jnp.float32)), axis=1)
    at = (coarse_ids // blk)[None, :] == jnp.arange(owners, dtype=jnp.int32)[:, None]
    gaps = (row_sq + jnp.sum(jnp.where(at, back, 0.0), axis=0)) / width
    return (new_fine, new_coarse, gaps)


def solution(mesh):
    fine_mesh = Mesh(mesh.devices.reshape(8, 4, 8, 2), DP + CENT)
    placed = (P(DP + CENT, None), P(DP + CENT), P(DP + CENT), P(), P(CENT, None, None))
    return jax.shard_map(
        body,
        mesh=fine_mesh,
        in_specs=placed,
        out_specs=(P(CENT, DP, None), P(), P(DP + CENT)),
        check_vma=False,
    )
```

time: 292 us -> 207 us (0.71)
  the two profiles are of different devices: /device:TPU:8 before, /device:TPU:1 now
where the time goes in v2:
time: 207 us; the launch traced here: 206 us
  blocking collectives  65.5 us (32%)
  waiting for transfers between devices  59.8 us (29%)
  Pallas kernels  31.4 us (15%)
  starting transfers between devices  21.1 us (10%)
  between operations  14.1 us (7%)
  other arithmetic  8.82 us (4%)
  local copies, waits for them, and re-layouts  3.61 us (2%)
    all_to_all x1, blocking collectives, body(): lax.all_to_all(coarse_part, DP, split_axis=0, concat_axis=0, tiled=True)  27.9 us
    all_gather x1, blocking collectives, body(): mine = jnp.sum(lax.all_gather(mine, CENT, axis=0, tiled=False), axis=0)  22.3 us
    all_to_all x1, waiting for transfers between devices, body(): lax.all_to_all(part, 'z', split_axis=0, concat_axis=0, tiled=True)  21.5 us
    all_to_all x1, waiting for transfers between devices, body(): lax.all_to_all(part, 'x', split_axis=0, concat_axis=0, tiled=True)  18.9 us
    pallas_call x1, Pallas kernels, fine_sums(): pl.pallas_call(sums_kernel, grid_spec=pltpu.PrefetchScalarGridSpec(num_sc...  16 us
    pallas_call x1, Pallas kernels, nearest(): pl.pallas_call(gaps_kernel, grid_spec=pltpu.PrefetchScalarGridSpec(num_sc...  15.4 us
    all_gather x1, blocking collectives, body(): sent = lax.all_gather(fine_ids, CENT, axis=0, tiled=False)  15.3 us
    all_gather x1, waiting for transfers between devices, body(): rows = lax.all_gather(embeds, CENT, axis=0, tiled=False)  12.4 us
  transfers between devices with their start and end apart: 5, of which 4 were waited for; matrix products, arithmetic and copies ran while one was open for 6% of the time, Pallas kernels for 15%

profile of v2, /device:TPU:1, one launch (start us, length us, event | category | flops | bytes accessed | tf_op | source)
XLA Modules:
  0.0 205.8 jit_solution(7827762085005601942)
XLA Ops:
  7.2 0.7 all-gather.7.cloned.1.call-update
  7.9 0.7 add_select_fusion.7
  8.6 0.1 fusion.9
  8.7 1.5 fusion
  10.2 0.1 reshape.218
  10.4 27.9 %all_to_all.25 = f32[32,4,896]{2,1,0:T(4,128)S(1)} all-to-all(f32[32,4,896]{2,1,0:T(4,128)S(1)} %reshape.218), channel_id=1, replica_groups=mesh['z'=8,'x'=4,'y'=8,'core'=2] {'z','x'}, dimensions={0} | all-to-all | bytes 917504 | tf_op jit(solution)/shard_map/all_to_all | solution.py:102
  38.4 22.3 %all-gather.4 = f32[16,4,896]{2,1,0:T(4,128)S(1)} all-gather(f32[1,4,896]{2,1,0:T(4,128)S(1)} %bitcast.38), channel_id=4, replica_groups=mesh['z'=8,'x'=4,'y'=8,'core'=2] {'y','core'}, dimensions={0}, use_global_device_ids=true | all-gather | bytes 243712 | tf_op jit(solution)/shard_map/all_gather | solution.py:103
  60.7 0.8 broadcast_in_dim.13
  61.5 4.1 %all-to-all-start.3 = ((f32[32,4,896]{2,1,0:T(4,128)}), f32[32,4,896]{2,1,0:T(4,128)S(1)}, u32[]{:S(2)}, u32[]{:S(2)}) async-start(f32[32,4,896]{2,1,0:T(4,128)} %broadcast_in_dim.13), calls=%async_computation.3 | async-start | bytes 917504 | tf_op jit(solution)/shard_map/all_to_all | solution.py:104
  65.7 15.3 %all-gather.3 = s32[16,1,512]{2,1,0:T(1,128)S(1)} all-gather(s32[1,1,512]{2,1,0:T(1,128)S(1)} %bitcast.40), channel_id=2, replica_groups=mesh['z'=8,'x'=4,'y'=8,'core'=2] {'y','core'}, dimensions={0}, use_global_device_ids=true | all-gather | bytes 34816 | tf_op jit(solution)/shard_map/all_gather | solution.py:94
  81.0 0.7 fusion.32
  81.7 0.6 broadcast_in_dim.12.key_ref
  82.3 0.7 fusion.16.target_ref
  83.1 12.4 %all-gather.7.cloned.1.call-done = bf16[8192,768]{1,0:T(8,128)(2,1)} async-done(((bf16[512,768]{1,0:T(8,128)(2,1)}), bf16[8192,768]{1,0:T(8,128)(2,1)}) %all-gather.7.cloned.1.call-update) | async-done | bytes 12582928 | tf_op jit(solution)/shard_map/all_gather | solution.py:93
  95.4 16.0 %shard_map.76 = f32[32,4,8,768]{3,2,1,0:T(8,128)} custom-call(s32[16]{0:T(128)} %get-tuple-element.6.pick, s32[16,1,512]{2,1,0:T(1,128)} %broadcast_in_dim.12.key_ref, s32[256,1]{1,0:T(8,128)} %fusion.16.target_ref, bf16[16,512,768]{2,1,0:T(8,128)(2,1)} %bitcast.35), custom_call_target="tpu_custom_call" | custom-call | flops 3221225472 | bytes 12582912 | tf_op jit(solution)/shard_map/pallas_call | solution.py:31
  111.4 0.8 copy-done.1
  112.2 4.0 %all-to-all-start = ((f32[4,8,32,768]{3,2,1,0:T(8,128)}), f32[4,8,32,768]{3,2,1,0:T(8,128)S(1)}, u32[]{:S(2)}, u32[]{:S(2)}) async-start(f32[4,8,32,768]{3,2,1,0:T(8,128)} %bitcast.37), calls=%async_computation | async-start | bytes 6291456 | tf_op jit(solution)/shard_map/all_to_all | solution.py:121
  116.2 1.8 multiply_reduce_fusion
  118.0 1.0 copy.12.square_ref
  119.0 15.4 %shard_map.77 = f32[16,1,512]{2,1,0:T(1,128)} custom-call(s32[16]{0:T(128)} %get-tuple-element.6.pick, bf16[8,128,768]{2,1,0:T(8,128)(2,1)} %cents_ref.1, f32[8,128,1]{2,1,0:T(8,128)} %copy.12.square_ref, bf16[16,512,768]{2,1,0:T(8,128)(2,1)} %bitcast.36), custom_call_target="tpu_custom_call" | custom-call | flops 1610612736 | bytes 12582912 | tf_op jit(solution)/shard_map/pallas_call | solution.py:61
  134.4 18.9 %all-to-all-done = f32[4,8,32,768]{3,2,1,0:T(8,128)S(1)} async-done(((f32[4,8,32,768]{3,2,1,0:T(8,128)}), f32[4,8,32,768]{3,2,1,0:T(8,128)S(1)}, u32[]{:S(2)}, u32[]{:S(2)}) %all-to-all-start) | async-done | bytes 3145760 | tf_op jit(solution)/shard_map/all_to_all | solution.py:121
  153.3 5.9 %all-to-all-start.4 = ((f32[16,1,512]{2,1,0:T(1,128)}), f32[16,1,512]{2,1,0:T(1,128)S(1)}, u32[]{:S(2)}, u32[]{:S(2)}) async-start(f32[16,1,512]{2,1,0:T(1,128)} %shard_map.77), calls=%async_computation.4 | async-start | bytes 65536 | tf_op jit(solution)/shard_map/all_to_all | solution.py:131
  159.2 1.1 reduce_sum.72
  160.3 6.3 %all-to-all-done.4 = f32[16,1,512]{2,1,0:T(1,128)S(1)} async-done(((f32[16,1,512]{2,1,0:T(1,128)}), f32[16,1,512]{2,1,0:T(1,128)S(1)}, u32[]{:S(2)}, u32[]{:S(2)}) %all-to-all-start.4) | async-done | bytes 32800 | tf_op jit(solution)/shard_map/all_to_all | solution.py:131
  166.6 7.1 %all-to-all-start.1 = ((f32[8,32,768]{2,1,0:T(8,128)}), f32[8,32,768]{2,1,0:T(8,128)S(1)}, u32[]{:S(2)}, u32[]{:S(2)}) async-start(f32[8,32,768]{2,1,0:T(8,128)} %reduce_sum.72), calls=%async_computation.1 | async-start | bytes 1572864 | tf_op jit(solution)/shard_map/all_to_all | solution.py:122
  173.7 0.2 multiply_reduce_fusion.1
  173.9 0.2 reshape.219
  174.1 0.1 slice_reduce_fusion
  174.3 0.8 fusion.4
  175.1 0.6 add_multiply_fusion
  175.7 21.5 %all-to-all-done.1 = f32[8,32,768]{2,1,0:T(8,128)S(1)} async-done(((f32[8,32,768]{2,1,0:T(8,128)}), f32[8,32,768]{2,1,0:T(8,128)S(1)}, u32[]{:S(2)}, u32[]{:S(2)}) %all-to-all-start.1) | async-done | bytes 786464 | tf_op jit(solution)/shard_map/all_to_all | solution.py:122
  197.3 1.6 add_divide_fusion
  (18 shorter events, 0.4 us)
Async XLA Ops:
  7.2 88.3 %all-gather.7.cloned.1.call-start = ((), (), s32[]{:S(2)}) async-start(), calls=%async_computation.5 | async-start | bytes 13369344 | tf_op jit(solution)/shard_map/all_gather | solution.py:93
  10.3 55.4 %copy-start.4 = (s32[512]{0:T(512)S(1)}, s32[512]{0:T(512)}, u32[]{:S(2)}) copy-start(s32[512]{0:T(512)} %param.7) | copy-start | bytes 6148
  61.5 49.9 %all-to-all-start.3 = ((f32[32,4,896]{2,1,0:T(4,128)}), f32[32,4,896]{2,1,0:T(4,128)S(1)}, u32[]{:S(2)}, u32[]{:S(2)}) async-start(f32[32,4,896]{2,1,0:T(4,128)} %broadcast_in_dim.13), calls=%async_computation.3 | async-start | bytes 917504 | tf_op jit(solution)/shard_map/all_to_all | solution.py:104
  111.4 0.8 copy-start.1
  112.2 41.1 %all-to-all-start = ((f32[4,8,32,768]{3,2,1,0:T(8,128)}), f32[4,8,32,768]{3,2,1,0:T(8,128)S(1)}, u32[]{:S(2)}, u32[]{:S(2)}) async-start(f32[4,8,32,768]{3,2,1,0:T(8,128)} %bitcast.37), calls=%async_computation | async-start | bytes 6291456 | tf_op jit(solution)/shard_map/all_to_all | solution.py:121
  153.3 13.3 %all-to-all-start.4 = ((f32[16,1,512]{2,1,0:T(1,128)}), f32[16,1,512]{2,1,0:T(1,128)S(1)}, u32[]{:S(2)}, u32[]{:S(2)}) async-start(f32[16,1,512]{2,1,0:T(1,128)} %shard_map.77), calls=%async_computation.4 | async-start | bytes 65536 | tf_op jit(solution)/shard_map/all_to_all | solution.py:131
  160.3 13.4 %copy-start = (bf16[512,768]{1,0:T(8,128)(2,1)S(1)}, bf16[512,768]{1,0:T(8,128)(2,1)}, u32[]{:S(2)}) copy-start(bf16[512,768]{1,0:T(8,128)(2,1)} %param.5) | copy-start | bytes 2359300
  160.3 13.6 %copy-start.2 = (f32[32,4,896]{2,1,0:T(4,128)S(1)}, f32[32,4,896]{2,1,0:T(4,128)}, u32[]{:S(2)}) copy-start(f32[32,4,896]{2,1,0:T(4,128)} %copy-done.1) | copy-start | bytes 1376260
  160.3 14.0 %copy-start.3 = (f32[128,768]{1,0:T(8,128)S(1)}, f32[128,768]{1,0:T(8,128)}, u32[]{:S(2)}) copy-start(f32[128,768]{1,0:T(8,128)} %param.8) | copy-start | bytes 1179652
  166.6 30.7 %all-to-all-start.1 = ((f32[8,32,768]{2,1,0:T(8,128)}), f32[8,32,768]{2,1,0:T(8,128)S(1)}, u32[]{:S(2)}, u32[]{:S(2)}) async-start(f32[8,32,768]{2,1,0:T(8,128)} %reduce_sum.72), calls=%async_computation.1 | async-start | bytes 1572864 | tf_op jit(solution)/shard_map/all_to_all | solution.py:122
Sparse Core Ops, SparseCore 0:
  10.1 85.2 all-gather.6

commit v3 on v2

v3 whole, which is shorter than its diff:
```python
import jax
import jax.numpy as jnp
from jax import lax
from jax.experimental import pallas as pl
from jax.experimental.pallas import tpu as pltpu
from jax.sharding import Mesh, PartitionSpec as P

COARSE = 128
DP = ("z", "x")
CENT = ("y", "core")
VMEM = 56 * 2**20


def sums_kernel(pick_ref, key_ref, target_ref, rows_ref, total, held, sems):
    sources = rows_ref.shape[0]

    def fetch(s):
        return pltpu.make_async_copy(rows_ref.at[s], held.at[s], sems.at[s])

    for s in range(sources):
        fetch(s).start()
    total[...] = jnp.zeros_like(total)

    @pl.loop(0, sources)
    def _(s):
        hot = (target_ref[...] == key_ref[s]).astype(jnp.bfloat16)
        fetch(s).wait()
        part = jnp.dot(hot, held[s], preferred_element_type=jnp.float32)
        total[:, pick_ref[s] // 2] += part.reshape(total.shape[0], 8, part.shape[1])


def fine_sums(pick, keys, target, rows):
    sources, per_source, width = rows.shape
    groups = target.shape[0] // 8
    shape = (groups, 4, 8, width)
    return pl.pallas_call(
        sums_kernel,
        in_specs=[
            pl.BlockSpec(memory_space=pltpu.SMEM),
            pl.BlockSpec(memory_space=pltpu.VMEM),
            pl.BlockSpec(memory_space=pltpu.VMEM),
            pl.BlockSpec(memory_space=pl.ANY),
        ],
        out_specs=pl.BlockSpec(memory_space=pltpu.VMEM),
        out_shape=jax.ShapeDtypeStruct(shape, jnp.float32),
        scratch_shapes=[
            pltpu.VMEM(rows.shape, rows.dtype),
            pltpu.SemaphoreType.DMA((sources,)),
        ],
        compiler_params=pltpu.CompilerParams(vmem_limit_bytes=VMEM),
        cost_estimate=pl.CostEstimate(
            flops=4 * groups * 4 * rows.size, bytes_accessed=2 * rows.size, transcendentals=0
        ),
    )(pick, keys, target, rows)


def gaps_kernel(pick_ref, cents_ref, square_ref, rows_ref, out_ref, held, sems):
    sources = rows_ref.shape[0]

    def fetch(s):
        return pltpu.make_async_copy(rows_ref.at[s], held.at[s], sems.at[s])

    for s in range(sources):
        fetch(s).start()

    @pl.loop(0, sources)
    def _(s):
        c = pick_ref[s]
        fetch(s).wait()
        dots = lax.dot_general(
            cents_ref[c], held[s], (((1,), (1,)), ((), ())), preferred_element_type=jnp.float32
        )
        out_ref[s] = jnp.min(square_ref[c] - 2.0 * dots, axis=0, keepdims=True)


def nearest(pick, cents, squares, rows):
    sources, per_source, width = rows.shape
    return pl.pallas_call(
        gaps_kernel,
        in_specs=[
            pl.BlockSpec(memory_space=pltpu.SMEM),
            pl.BlockSpec(memory_space=pltpu.VMEM),
            pl.BlockSpec(memory_space=pltpu.VMEM),
            pl.BlockSpec(memory_space=pl.ANY),
        ],
        out_specs=pl.BlockSpec(memory_space=pltpu.VMEM),
        out_shape=jax.ShapeDtypeStruct((sources, 1, per_source), jnp.float32),
        scratch_shapes=[
            pltpu.VMEM(rows.shape, rows.dtype),
            pltpu.SemaphoreType.DMA((sources,)),
        ],
        compiler_params=pltpu.CompilerParams(vmem_limit_bytes=VMEM),
        cost_estimate=pl.CostEstimate(
            flops=2 * cents.shape[1] * rows.size, bytes_accessed=2 * rows.size, transcendentals=0
        ),
    )(pick, cents, squares, rows)


def body(embeds, coarse_ids, fine_ids, coarse_cents, fine_cents):
    blk, per, width = fine_cents.shape
    count = embeds.shape[0]
    planes = lax.axis_size(DP)
    owners = lax.axis_size(CENT)
    share = per // planes
    me = lax.axis_index(CENT)
    anchor_coarse = count * planes * owners // COARSE
    anchor_fine = max(1, anchor_coarse // per)
    local = fine_ids - coarse_ids * per

    rows = lax.all_gather(embeds, CENT, axis=0, tiled=False)
    sent = lax.all_gather(fine_ids, CENT, axis=0, tiled=False)

    coarse_hot = (jnp.arange(COARSE, dtype=jnp.int32)[:, None] == coarse_ids[None, :]).astype(jnp.bfloat16)
    fine_hot = (local[:, None] == jnp.arange(per, dtype=jnp.int32)[None, :]).astype(jnp.bfloat16)
    coarse_part = jnp.dot(
        coarse_hot, jnp.concatenate([embeds, fine_hot], axis=1), preferred_element_type=jnp.float32
    )
    largest = jnp.broadcast_to(jnp.max(jnp.abs(embeds)).astype(jnp.float32), (COARSE, 128))
    both = width + per
    coarse_part = jnp.concatenate([coarse_part, largest], axis=1).reshape(planes, COARSE // planes, both + 128)
    heard = lax.all_to_all(coarse_part, DP, split_axis=0, concat_axis=0, tiled=True)
    mine = jnp.concatenate([jnp.sum(heard[:, :, :both], axis=0), jnp.max(heard[:, :, both:], axis=0)], axis=1)
    heard = lax.all_gather(mine, CENT, axis=0, tiled=False)
    mine = jnp.sum(heard[:, :, :both], axis=0)
    largest = jnp.max(heard[:, :, both:])
    totals = lax.all_to_all(
        jnp.broadcast_to(mine[None], (planes,) + mine.shape), DP, split_axis=0, concat_axis=0, tiled=True
    ).reshape(COARSE, both)
    counts = totals[:, width:]
    new_coarse = (anchor_coarse * coarse_cents + totals[:, :width]) / (
        anchor_coarse + jnp.sum(counts, axis=1, keepdims=True)
    )

    powers = jnp.asarray([2.0**k for k in range(-8, 101)], jnp.float32)
    scale = jnp.max(jnp.where(powers * largest <= 60000.0 / (owners * 128), powers, powers[0]))

    cluster = sent // per - me * blk
    ours = (cluster >= 0) & (cluster < blk)
    pick = jnp.max(jnp.where(ours, cluster, 0), axis=1)
    keys = jnp.where(ours, sent % (2 * per), -1)[:, None, :]
    slot = jnp.arange(2 * per, dtype=jnp.int32)
    target = ((slot // share) % 2 * per + slot // (2 * share) * share + slot % share)[:, None]

    part = fine_sums(pick, keys, target, rows).reshape(planes, blk * share, width)
    part = (part * scale).astype(jnp.float16)
    part = lax.all_to_all(part, DP, split_axis=0, concat_axis=0, tiled=True)
    fine_sum = (jnp.sum(part.astype(jnp.float32), axis=0) * (1.0 / scale)).reshape(blk, share, width)
    first = lax.axis_index(DP) * share
    former = lax.dynamic_slice_in_dim(fine_cents, first, share, 1).astype(jnp.float32)
    fine_num = lax.dynamic_slice(counts, (me * blk, first), (blk, share))
    new_fine = (anchor_fine * former + fine_sum) / (anchor_fine + fine_num[:, :, None])

    squares = jnp.sum(jnp.square(fine_cents.astype(jnp.float32)), axis=2, keepdims=True)
    least = nearest(pick, fine_cents, squares, rows)[:, 0]
    back = lax.all_gather(least, CENT, axis=0, tiled=False)
    back = lax.dynamic_index_in_dim(back, me, 1, keepdims=False)
    row_sq = jnp.sum(jnp.square(embeds.astype(jnp.float32)), axis=1)
    at = (coarse_ids // blk)[None, :] == jnp.arange(owners, dtype=jnp.int32)[:, None]
    gaps = (row_sq + jnp.sum(jnp.where(at, back, 0.0), axis=0)) / width
    return (new_fine, new_coarse, gaps)


def solution(mesh):
    fine_mesh = Mesh(mesh.devices.reshape(8, 4, 8, 2), DP + CENT)
    placed = (P(DP + CENT, None), P(DP + CENT), P(DP + CENT), P(), P(CENT, None, None))
    return jax.shard_map(
        body,
        mesh=fine_mesh,
        in_specs=placed,
        out_specs=(P(CENT, DP, None), P(), P(DP + CENT)),
        check_vma=False,
    )
```

time: 207 us -> 171 us (0.83)
  waiting for transfers between devices: 59.8 us -> 25.3 us
  blocking collectives: 65.5 us -> 55 us
  starting transfers between devices: 21.1 us -> 31.6 us
  Pallas kernels: 31.4 us -> 21.3 us
  other arithmetic: 8.82 us -> 15.5 us
    all_to_all x3 -> x2, waiting for transfers between devices: 46.7 us -> 6.34 us  [the longest x1 6.33 us: body(): part = lax.all_to_all(part, DP, split_axis=0, concat_axis=0, tiled=True)]
    all_to_all x1 -> x0, blocking collectives: 27.9 us -> none  [body(): lax.all_to_all(coarse_part, DP, split_axis=0, concat_axis=0, tiled=True)]
    all_gather x1 -> x2, blocking collectives: 22.3 us -> 36.5 us  [the longest x1 18.9 us: body(): heard = lax.all_gather(mine, CENT, axis=0, tiled=False)]
    pallas_call x2, Pallas kernels: 31.4 us -> 21.3 us  [the longest x1 11.4 us: fine_sums(): pl.pallas_call(sums_kernel, in_specs=[pl.BlockSpec(memory_space=pltpu.SME...]
    all_to_all x3 -> x2, starting transfers between devices: 16.9 us -> 24 us  [the longest x1 13.8 us: body(): lax.all_to_all(coarse_part, DP, split_axis=0, concat_axis=0, tiled=True)]
    all_gather x1, waiting for transfers between devices: 12.4 us -> 18.3 us  [body(): rows = lax.all_gather(embeds, CENT, axis=0, tiled=False)]
    convert_element_type x0 -> x1, other arithmetic: none -> 3.94 us  [body(): part = (part * scale).astype(jnp.float16)]
    reduce_max x0 -> x4, other arithmetic: none -> 3.7 us  [the longest x1 1.84 us: body(): jnp.max(jnp.abs(embeds)).astype(jnp.float32)]
  transfers between devices with their start and end apart: 5 -> 4, of which waited for: 4 -> 2; matrix products, arithmetic and copies ran while one was open for 6% -> 11% of each run, Pallas kernels for 15% -> 13%
where the time goes in v3:
time: 171 us; the launch traced here: 169 us
  blocking collectives  55 us (32%)
  starting transfers between devices  31.6 us (18%)
  waiting for transfers between devices  25.3 us (15%)
  Pallas kernels  21.3 us (12%)
  other arithmetic  15.5 us (9%)
  between operations  14.8 us (9%)
  local copies, waits for them, and re-layouts  4.45 us (3%)
    all_gather x1, blocking collectives, body(): heard = lax.all_gather(mine, CENT, axis=0, tiled=False)  18.9 us
    all_gather x1, blocking collectives, body(): sent = lax.all_gather(fine_ids, CENT, axis=0, tiled=False)  18.5 us
    all_gather x1, waiting for transfers between devices, body(): rows = lax.all_gather(embeds, CENT, axis=0, tiled=False)  18.3 us
    all_gather x1, blocking collectives, body(): back = lax.all_gather(least, CENT, axis=0, tiled=False)  17.6 us
    all_to_all x1, starting transfers between devices, body(): lax.all_to_all(coarse_part, DP, split_axis=0, concat_axis=0, tiled=True)  13.8 us
    pallas_call x1, Pallas kernels, fine_sums(): pl.pallas_call(sums_kernel, in_specs=[pl.BlockSpec(memory_space=pltpu.SME...  11.4 us
    all_to_all x1, starting transfers between devices, body(): part = lax.all_to_all(part, DP, split_axis=0, concat_axis=0, tiled=True)  10.1 us
    pallas_call x1, Pallas kernels, nearest(): pl.pallas_call(gaps_kernel, in_specs=[pl.BlockSpec(memory_space=pltpu.SME...  9.88 us
  transfers between devices with their start and end apart: 4, of which 2 were waited for; matrix products, arithmetic and copies ran while one was open for 11% of the time, Pallas kernels for 13%

profile of v3, /device:TPU:1, one launch (start us, length us, event | category | flops | bytes accessed | tf_op | source)
XLA Modules:
  0.0 169.3 jit_solution(12987917338118570218)
XLA Ops:
  7.2 0.7 all-gather.8.cloned.1.call-update
  7.9 1.8 %abs_reduce_fusion = bf16[]{:T(256)} fusion(bf16[512,768]{1,0:T(8,128)(2,1)} %param.6), kind=kLoop, calls=%fused_computation.9 | loop fusion | flops 786431 | bytes 786434 | tf_op jit(solution)/shard_map/reduce_max | solution.py:118
  9.7 0.7 add_select_fusion.5
  10.4 0.1 fusion.10
  10.6 1.5 fusion.1
  12.1 0.7 concatenate.10
  12.8 1.0 reshape.148
  13.7 13.8 %all-to-all-start = ((f32[32,4,1024]{2,1,0:T(4,128)}), f32[32,4,1024]{2,1,0:T(4,128)S(1)}, u32[]{:S(2)}, u32[]{:S(2)}) async-start(f32[32,4,1024]{2,1,0:T(4,128)} %reshape.148), calls=%async_computation | async-start | bytes 1048576 | tf_op jit(solution)/shard_map/all_to_all | solution.py:121
  27.6 18.5 %all-gather.4 = s32[16,1,512]{2,1,0:T(1,128)S(1)} all-gather(s32[1,1,512]{2,1,0:T(1,128)S(1)} %bitcast.42), channel_id=2, replica_groups=mesh['z'=8,'x'=4,'y'=8,'core'=2] {'y','core'}, dimensions={0}, use_global_device_ids=true | all-gather | bytes 34816 | tf_op jit(solution)/shard_map/all_gather | solution.py:111
  46.1 0.7 fusion.24
  46.9 18.9 %all-gather.5 = f32[16,4,1024]{2,1,0:T(4,128)S(1)} all-gather(f32[1,4,1024]{2,1,0:T(4,128)S(1)} %maximum_bitcast_fusion), channel_id=4, replica_groups=mesh['z'=8,'x'=4,'y'=8,'core'=2] {'y','core'}, dimensions={0}, use_global_device_ids=true | all-gather | bytes 278528 | tf_op jit(solution)/shard_map/all_gather | solution.py:123
  65.8 0.8 broadcast_in_dim.18
  66.7 7.5 %all-to-all-start.2 = ((f32[32,4,896]{2,1,0:T(4,128)}), f32[32,4,896]{2,1,0:T(4,128)S(1)}, u32[]{:S(2)}, u32[]{:S(2)}) async-start(f32[32,4,896]{2,1,0:T(4,128)} %broadcast_in_dim.18), calls=%async_computation.2 | async-start | bytes 917504 | tf_op jit(solution)/shard_map/all_to_all | solution.py:126
  74.2 0.7 fusion.16.target_ref
  74.9 0.6 broadcast_in_dim.16.key_ref
  75.5 0.6 slice_reduce_fusion.3
  76.2 1.2 fusion.30
  77.4 18.3 %all-gather.8.cloned.1.call-done = bf16[8192,768]{1,0:T(8,128)(2,1)} async-done(((bf16[512,768]{1,0:T(8,128)(2,1)}), bf16[8192,768]{1,0:T(8,128)(2,1)}) %all-gather.8.cloned.1.call-update) | async-done | bytes 12582928 | tf_op jit(solution)/shard_map/all_gather | solution.py:110
  95.6 11.4 %shard_map.85 = f32[32,4,8,768]{3,2,1,0:T(8,128)} custom-call(s32[16]{0:T(128)} %get-tuple-element.6.pick_ref, s32[16,1,512]{2,1,0:T(1,128)} %broadcast_in_dim.16.key_ref, s32[256,1]{1,0:T(8,128)} %fusion.16.target_ref, bf16[16,512,768]{2,1,0:T(8,128)(2,1)} %bitcast.38), custom_call_target="tpu_custom_call" | custom-call | flops 3221225472 | bytes 12582912 | tf_op jit(solution)/shard_map/pallas_call | solution.py:36
  107.0 3.9 %fusion = f16[32,32,768]{2,1,0:T(8,128)(2,1)} fusion(f32[32,4,8,768]{3,2,1,0:T(8,128)} %shard_map.85, f32[]{:T(128)} %fusion.30), kind=kLoop, calls=%fused_computation.3 | loop fusion | flops 1572864 | bytes 4718596 | tf_op jit(solution)/shard_map/convert_element_type | solution.py:145
  111.0 10.1 %all-to-all-start.1 = ((f16[32,32,768]{2,1,0:T(8,128)(2,1)}), f16[32,32,768]{2,1,0:T(8,128)(2,1)}, u32[]{:S(2)}, u32[]{:S(2)}) async-start(f16[32,32,768]{2,1,0:T(8,128)(2,1)} %fusion), calls=%async_computation.1 | async-start | bytes 3145728 | tf_op jit(solution)/shard_map/all_to_all | solution.py:146
  121.2 0.4 multiply_reduce_fusion
  121.5 1.0 copy.10.square_ref
  122.6 0.2 multiply_reduce_fusion.1
  123.4 0.2 reshape.149
  123.8 0.8 fusion.5
  124.6 9.9 %shard_map.86 = f32[16,1,512]{2,1,0:T(1,128)} custom-call(s32[16]{0:T(128)} %get-tuple-element.6.pick_ref, bf16[8,128,768]{2,1,0:T(8,128)(2,1)} %cents_ref.1, f32[8,128,1]{2,1,0:T(8,128)} %copy.10.square_ref, bf16[16,512,768]{2,1,0:T(8,128)(2,1)} %bitcast.39), custom_call_target="tpu_custom_call" | custom-call | flops 1610612736 | bytes 12582912 | tf_op jit(solution)/shard_map/pallas_call | solution.py:78
  134.5 17.6 %all-gather.3 = f32[256,1,512]{2,1,0:T(1,128)S(1)} all-gather(f32[16,1,512]{2,1,0:T(1,128)} %shard_map.86), channel_id=5, replica_groups=mesh['z'=8,'x'=4,'y'=8,'core'=2] {'y','core'}, dimensions={0}, use_global_device_ids=true | all-gather | bytes 557056 | tf_op jit(solution)/shard_map/all_gather | solution.py:155
  152.2 0.6 add_multiply_fusion
  152.8 6.3 %all-to-all-done.1 = f16[32,32,768]{2,1,0:T(8,128)(2,1)} async-done(((f16[32,32,768]{2,1,0:T(8,128)(2,1)}), f16[32,32,768]{2,1,0:T(8,128)(2,1)}, u32[]{:S(2)}, u32[]{:S(2)}) %all-to-all-start.1) | async-done | bytes 1572896 | tf_op jit(solution)/shard_map/all_to_all | solution.py:146
  159.1 1.6 convert_reduce_fusion
  160.8 1.6 add_divide_fusion
  (25 shorter events, 0.5 us)
Async XLA Ops:
  7.2 88.5 %all-gather.8.cloned.1.call-start = ((), (), s32[]{:S(2)}) async-start(), calls=%async_computation.3 | async-start | bytes 13369344 | tf_op jit(solution)/shard_map/all_gather | solution.py:110
  12.0 15.6 %copy-start.3 = (s32[512]{0:T(512)S(1)}, s32[512]{0:T(512)}, u32[]{:S(2)}) copy-start(s32[512]{0:T(512)} %param.8) | copy-start | bytes 6148
  13.7 62.5 %copy-start.4 = (f32[109]{0:T(128)S(1)}, f32[109]{0:T(128)}, u32[]{:S(2)}) copy-start(f32[109]{0:T(128)} %constant.142.clone) | copy-start | bytes 1312
  13.7 33.0 %all-to-all-start = ((f32[32,4,1024]{2,1,0:T(4,128)}), f32[32,4,1024]{2,1,0:T(4,128)S(1)}, u32[]{:S(2)}, u32[]{:S(2)}) async-start(f32[32,4,1024]{2,1,0:T(4,128)} %reshape.148), calls=%async_computation | async-start | bytes 1048576 | tf_op jit(solution)/shard_map/all_to_all | solution.py:121
  66.7 44.3 %all-to-all-start.2 = ((f32[32,4,896]{2,1,0:T(4,128)}), f32[32,4,896]{2,1,0:T(4,128)S(1)}, u32[]{:S(2)}, u32[]{:S(2)}) async-start(f32[32,4,896]{2,1,0:T(4,128)} %broadcast_in_dim.18), calls=%async_computation.2 | async-start | bytes 917504 | tf_op jit(solution)/shard_map/all_to_all | solution.py:126
  111.0 10.2 %copy-start.1 = (bf16[8,128,768]{2,1,0:T(8,128)(2,1)S(1)}, bf16[8,128,768]{2,1,0:T(8,128)(2,1)}, u32[]{:S(2)}) copy-start(bf16[8,128,768]{2,1,0:T(8,128)(2,1)} %cents_ref.1) | copy-start | bytes 4718596
  111.0 48.2 %all-to-all-start.1 = ((f16[32,32,768]{2,1,0:T(8,128)(2,1)}), f16[32,32,768]{2,1,0:T(8,128)(2,1)}, u32[]{:S(2)}, u32[]{:S(2)}) async-start(f16[32,32,768]{2,1,0:T(8,128)(2,1)} %fusion), calls=%async_computation.1 | async-start | bytes 3145728 | tf_op jit(solution)/shard_map/all_to_all | solution.py:146
  121.1 1.5 copy-start
  121.1 2.6 %copy-start.2 = (f32[128,768]{1,0:T(8,128)S(1)}, f32[128,768]{1,0:T(8,128)}, u32[]{:S(2)}) copy-start(f32[128,768]{1,0:T(8,128)} %param.9) | copy-start | bytes 1179652
Sparse Core Ops, SparseCore 0:
  10.1 85.4 all-gather.7

commit v4 on v3

v4 whole, which is shorter than its diff:
```python
import functools

import jax
import jax.numpy as jnp
from jax import lax
from jax.experimental import pallas as pl
from jax.experimental.pallas import tpu as pltpu
from jax.sharding import Mesh, PartitionSpec as P

COARSE = 128
DP = ("z", "x")
CENT = ("y", "core")
STEPS = 13
VMEM = 56 * 2**20


def message_kernel(share, owned, coarse_ref, fine_ref, rows_ref, out_ref):
    count, width = rows_ref.shape
    per = 128
    lines = out_ref.shape[0]
    slots, chunk = 8, 4
    full, half = share * width, width // 2
    coarse = coarse_ref[...]
    local = fine_ref[...] - coarse * per
    owner = coarse // owned

    owners = lax.broadcasted_iota(jnp.int32, (16, count), 0)
    present = jnp.max((owners == owner).astype(jnp.int32), axis=1, keepdims=True)
    slot_row = jnp.sum(jnp.where(owners < owner, present, 0), axis=0, keepdims=True)
    slot_ids = lax.broadcasted_iota(jnp.int32, (slots, count), 0)
    cluster = jnp.max(jnp.where(slot_ids == slot_row, coarse, 0), axis=1, keepdims=True)

    largest = jnp.max(jnp.abs(rows_ref[...]).astype(jnp.float32))
    scale, step = 1.0, 0.0
    for k in range(1, STEPS):
        fits = largest * 256.0**k <= 60000.0 / count
        scale = jnp.where(fits, 256.0**k, scale)
        step = jnp.where(fits, float(k), step)

    line = lax.broadcasted_iota(jnp.int32, (lines, 1), 0)
    key = slot_row * per + local
    target = (line % slots) * per + (line // slots) * share
    for j in range(share):
        hot = (target + j == key).astype(jnp.bfloat16)
        part = jnp.dot(hot, rows_ref[...], preferred_element_type=jnp.float32)
        out_ref[:, j * width : (j + 1) * width] = part * scale
    upper = line % slots < chunk
    hot = ((line // slots) * chunk + line % chunk == coarse).astype(jnp.bfloat16)
    part = jnp.dot(hot, rows_ref[...], preferred_element_type=jnp.float32)
    out_ref[:, full : full + half] = jnp.where(upper, part[:, :half], part[:, half:]) * scale
    fine_hot = (lax.broadcasted_iota(jnp.int32, (per, count), 0) == local).astype(jnp.bfloat16)
    numbers = lax.dot_general(hot, fine_hot, (((1,), (1,)), ((), ())), preferred_element_type=jnp.float32)
    lane = lax.broadcasted_iota(jnp.int32, (chunk, per), 1)
    cluster = cluster.astype(jnp.float32)
    notes = jnp.where(lane < 32, cluster[:chunk], jnp.where(lane < 64, cluster[chunk:], step))
    notes = jnp.concatenate([notes, notes], axis=0)
    notes = jnp.broadcast_to(notes[None], (lines // slots, slots, per)).reshape(lines, per)
    out_ref[:, full + half :] = jnp.where(upper, numbers, notes)


def message_of(coarse_ids, fine_ids, rows, planes, share, owned):
    width = rows.shape[1]
    shape = (planes * 8, share * width + width // 2 + 128)
    return pl.pallas_call(
        functools.partial(message_kernel, share, owned),
        in_specs=[pl.BlockSpec(memory_space=pltpu.VMEM)] * 3,
        out_specs=pl.BlockSpec(memory_space=pltpu.VMEM),
        out_shape=jax.ShapeDtypeStruct(shape, jnp.float32),
        compiler_params=pltpu.CompilerParams(vmem_limit_bytes=VMEM),
        cost_estimate=pl.CostEstimate(
            flops=2 * shape[0] * shape[1] * rows.shape[0], bytes_accessed=16 * rows.size, transcendentals=0
        ),
    )(coarse_ids[None, :], fine_ids[None, :], rows)


def gaps_kernel(pick_ref, cents_ref, square_ref, rows_ref, out_ref, held, sems):
    sources = rows_ref.shape[0]

    def fetch(s):
        return pltpu.make_async_copy(rows_ref.at[s], held.at[s], sems.at[s])

    for s in range(sources):
        fetch(s).start()

    @pl.loop(0, sources, unroll=4)
    def _(s):
        c = pick_ref[s]
        fetch(s).wait()
        dots = lax.dot_general(
            cents_ref[c], held[s], (((1,), (1,)), ((), ())), preferred_element_type=jnp.float32
        )
        out_ref[s] = jnp.min(square_ref[c] - 2.0 * dots, axis=0, keepdims=True)


def nearest(pick, cents, squares, rows):
    sources, per_source, width = rows.shape
    return pl.pallas_call(
        gaps_kernel,
        in_specs=[
            pl.BlockSpec(memory_space=pltpu.SMEM),
            pl.BlockSpec(memory_space=pltpu.VMEM),
            pl.BlockSpec(memory_space=pltpu.VMEM),
            pl.BlockSpec(memory_space=pl.ANY),
        ],
        out_specs=pl.BlockSpec(memory_space=pltpu.VMEM),
        out_shape=jax.ShapeDtypeStruct((sources, 1, per_source), jnp.float32),
        scratch_shapes=[
            pltpu.VMEM(rows.shape, rows.dtype),
            pltpu.SemaphoreType.DMA((sources,)),
        ],
        compiler_params=pltpu.CompilerParams(vmem_limit_bytes=VMEM),
        cost_estimate=pl.CostEstimate(
            flops=2 * cents.shape[1] * rows.size, bytes_accessed=2 * rows.size, transcendentals=0
        ),
    )(pick, cents, squares, rows)


def after(value, earlier):
    return value + (earlier[(0,) * earlier.ndim].astype(jnp.float32) * 0.0).astype(value.dtype)


def body(embeds, coarse_ids, fine_ids, coarse_cents, fine_cents):
    blk, per, width = fine_cents.shape
    count = embeds.shape[0]
    planes = lax.axis_size(DP)
    owners = lax.axis_size(CENT)
    share = per // planes
    chunk = COARSE // planes
    slots = 8
    me = lax.axis_index(CENT)
    core = lax.axis_index("core")
    anchor_coarse = count * planes * owners // COARSE
    anchor_fine = max(1, anchor_coarse // per)

    rows = lax.all_gather(embeds, CENT, axis=0, tiled=False)

    message = message_of(coarse_ids, fine_ids, embeds, planes, share, blk)
    heard = message.astype(jnp.float16).reshape(planes, slots, -1)
    heard = lax.all_to_all(heard, DP, split_axis=0, concat_axis=0, tiled=True)
    sent = lax.all_gather(after(coarse_ids, message), CENT, axis=0, tiled=False)

    full, half = share * width, width // 2
    notes = after(heard[:, chunk:, full + half :].astype(jnp.float32), sent)
    from_step = notes[:, 0, per - 1]
    from_cluster = jnp.concatenate([notes[:, :, 0], notes[:, :, 32]], axis=1).astype(jnp.int32)
    back_scale = jnp.zeros_like(from_step)
    for k in range(STEPS):
        back_scale = jnp.where(from_step == k, 256.0**-k, back_scale)
    weights = jnp.where(
        jnp.arange(COARSE, dtype=jnp.int32)[:, None, None] == from_cluster[None], back_scale[None, :, None], 0.0
    )
    weights = weights.reshape(COARSE, planes * slots).astype(jnp.bfloat16)
    values = heard[:, :, :full].reshape(planes * slots, full).astype(jnp.float32)
    high = lax.reduce_precision(values, 8, 7)
    low = (values - high).astype(jnp.bfloat16)
    high = high.astype(jnp.bfloat16)
    table = jnp.dot(weights, high, preferred_element_type=jnp.float32) + jnp.dot(
        weights, low, preferred_element_type=jnp.float32
    )

    rest = heard[:, :, full:].astype(jnp.float32)
    factor = jnp.where(jnp.arange(rest.shape[2])[None, None, :] < half, back_scale[:, None, None], 1.0)
    rest = jnp.sum(rest * factor, axis=0)

    table = table.reshape(owners // 2, 2, blk, full)
    kept = lax.dynamic_index_in_dim(table, core, 1, keepdims=False)
    given = lax.dynamic_index_in_dim(table, 1 - core, 1, keepdims=False)
    kept = jnp.concatenate([kept, jnp.broadcast_to(rest[None], (owners // 2,) + rest.shape)], axis=2)
    given = jnp.concatenate([given, jnp.broadcast_to(rest[None], (owners // 2,) + rest.shape)], axis=2)
    both = kept + lax.ppermute(given, "core", [(0, 1), (1, 0)])
    arrived = lax.all_to_all(both, "y", split_axis=0, concat_axis=0, tiled=True)

    near = sent - me * blk
    pick = jnp.max(jnp.where((near >= 0) & (near < blk), near, 0), axis=1)
    squares = jnp.sum(jnp.square(fine_cents.astype(jnp.float32)), axis=2, keepdims=True)
    least = nearest(after(pick, both), fine_cents, squares, rows)[:, 0]

    both_sum = jnp.sum(after(arrived, least), axis=0)
    fine_sum = both_sum[:, :full].reshape(blk, share, width)
    rest = both_sum[:, full:]
    mine = jnp.concatenate([rest[:chunk, :half], rest[chunk:, :half], rest[:chunk, half:]], axis=1)
    totals = lax.all_to_all(
        jnp.broadcast_to(mine[None], (planes,) + mine.shape), DP, split_axis=0, concat_axis=0, tiled=True
    ).reshape(COARSE, width + per)
    back = lax.all_gather(after(least, mine), CENT, axis=0, tiled=False)
    back = lax.dynamic_index_in_dim(back, me, 1, keepdims=False)
    totals = after(totals, back)
    counts = totals[:, width:]
    new_coarse = (anchor_coarse * coarse_cents + totals[:, :width]) / (
        anchor_coarse + jnp.sum(counts, axis=1, keepdims=True)
    )
    first = lax.axis_index(DP) * share
    former = lax.dynamic_slice_in_dim(fine_cents, first, share, 1).astype(jnp.float32)
    fine_num = lax.dynamic_slice(counts, (me * blk, first), (blk, share))
    new_fine = (anchor_fine * former + fine_sum) / (anchor_fine + fine_num[:, :, None])

    row_sq = jnp.sum(jnp.square(embeds.astype(jnp.float32)), axis=1)
    at = (coarse_ids // blk)[None, :] == jnp.arange(owners, dtype=jnp.int32)[:, None]
    gaps = (row_sq + jnp.sum(jnp.where(at, back, 0.0), axis=0)) / width
    return (new_fine, new_coarse, gaps)


def solution(mesh):
    fine_mesh = Mesh(mesh.devices.reshape(8, 4, 8, 2), DP + CENT)
    placed = (P(DP + CENT, None), P(DP + CENT), P(DP + CENT), P(), P(CENT, None, None))
    return jax.shard_map(
        body,
        mesh=fine_mesh,
        in_specs=placed,
        out_specs=(P(CENT, DP, None), P(), P(DP + CENT)),
        check_vma=False,
    )
```

time: 171 us -> 158 us (0.924)
  blocking collectives: 55 us -> 36 us
  waiting for transfers between devices: 25.3 us -> 34.9 us
  Pallas kernels: 21.3 us -> 14.3 us
  other arithmetic: 15.5 us -> 9.93 us
  local copies, waits for them, and re-layouts: 4.45 us -> 8.17 us
  starting transfers between devices: 31.6 us -> 35 us
  between operations: 14.8 us -> 18.2 us
    all_to_all x2, waiting for transfers between devices: 6.34 us -> 31.7 us  [the longest x1 21.5 us: body(): heard = lax.all_to_all(heard, DP, split_axis=0, concat_axis=0, tiled=True)]
    all_gather x3 -> x2, blocking collectives: 55 us -> 36 us  [the longest x1 18.5 us: body(): sent = lax.all_gather(after(coarse_ids, message), CENT, axis=0, tiled=False)]
    all_gather x1, waiting for transfers between devices: 18.3 us -> 0.18 us  [body(): rows = lax.all_gather(embeds, CENT, axis=0, tiled=False)]
    pallas_call x1, Pallas kernels: 11.4 us -> 4.46 us  [message_of(): pl.pallas_call(functools.partial(message_kernel, share, owned), in_specs=...]
    slice x0 -> x13, local copies, waits for them, and re-layouts: none -> 4.75 us  [the longest x6 4.44 us: after(): earlier[(0,) * earlier.ndim].astype(jnp.float32) * 0.0]
    ppermute x0 -> x1, starting transfers between devices: none -> 4.42 us  [body(): both = kept + lax.ppermute(given, 'core', [(0, 1), (1, 0)])]
    convert_element_type x2 -> x1, other arithmetic: 4.07 us -> 0.01 us  [body(): jnp.concatenate([notes[:, :, 0], notes[:, :, 32]], axis=1).astype(jnp.int32)]
    reduce_max x4 -> x1, other arithmetic: 3.7 us -> 0.12 us  [body(): pick = jnp.max(jnp.where((near >= 0) & (near < blk), near, 0), axis=1)]
  transfers between devices with their start and end apart: 4 -> 5, of which waited for: 2 -> 4; matrix products, arithmetic and copies ran while one was open for 11% -> 9% of each run, Pallas kernels for 13% -> 9%
where the time goes in v4:
time: 158 us
  blocking collectives  36 us (23%)
  starting transfers between devices  35 us (22%)
  waiting for transfers between devices  34.9 us (22%)
  between operations  18.2 us (12%)
  Pallas kernels  14.3 us (9%)
  other arithmetic  9.93 us (6%)
  local copies, waits for them, and re-layouts  8.17 us (5%)
    all_to_all x1, waiting for transfers between devices, body(): heard = lax.all_to_all(heard, DP, split_axis=0, concat_axis=0, tiled=True)  21.5 us
    all_gather x1, blocking collectives, body(): sent = lax.all_gather(after(coarse_ids, message), CENT, axis=0, tiled=False)  18.5 us
    all_gather x1, blocking collectives, body(): back = lax.all_gather(after(least, mine), CENT, axis=0, tiled=False)  17.5 us
    all_to_all x1, starting transfers between devices, body(): heard = lax.all_to_all(heard, DP, split_axis=0, concat_axis=0, tiled=True)  13.8 us
    all_to_all x1, waiting for transfers between devices, body(): arrived = lax.all_to_all(both, 'y', split_axis=0, concat_axis=0, tiled=True)  10.2 us
    all_to_all x1, starting transfers between devices, body(): lax.all_to_all(jnp.broadcast_to(mine[None], (planes,) + mine.shape), DP,...  10 us
    pallas_call x1, Pallas kernels, nearest(): pl.pallas_call(gaps_kernel, in_specs=[pl.BlockSpec(memory_space=pltpu.SME...  9.88 us
    all_to_all x1, starting transfers between devices, body(): arrived = lax.all_to_all(both, 'y', split_axis=0, concat_axis=0, tiled=True)  6.67 us
  transfers between devices with their start and end apart: 5, of which 4 were waited for; matrix products, arithmetic and copies ran while one was open for 9% of the time, Pallas kernels for 9%

profile of v4, /device:TPU:1, one launch (start us, length us, event | category | flops | bytes accessed | tf_op | source)
XLA Modules:
  0.0 157.6 jit_solution(9751059030093001506)
XLA Ops:
  7.2 0.7 all-gather.6.cloned.1.call-update
  7.9 4.5 %shard_map.76 = f32[256,3584]{1,0:T(8,128)} custom-call(s32[1,512]{1,0:T(1,128)} %bitcast.60, s32[1,512]{1,0:T(1,128)} %bitcast.64, bf16[512,768]{1,0:T(8,128)(2,1)} %rows_ref.1), custom_call_target="tpu_custom_call" | custom-call | flops 939524096 | bytes 6291456 | tf_op jit(solution)/shard_map/pallas_call | solution.py:64
  12.4 3.5 %convert_bitcast_fusion = f16[32,8,3584]{2,1,0:T(8,128)(2,1)} fusion(f32[256,3584]{1,0:T(8,128)} %shard_map.76), kind=kLoop, calls=%fused_computation.5 | loop fusion | flops 917504 | bytes 5505024 | tf_op jit(solution)/shard_map/reshape | solution.py:138
  15.8 13.8 %all-to-all-start = ((f16[32,8,3584]{2,1,0:T(8,128)(2,1)}), f16[32,8,3584]{2,1,0:T(8,128)(2,1)S(1)}, u32[]{:S(2)}, u32[]{:S(2)}) async-start(f16[32,8,3584]{2,1,0:T(8,128)(2,1)} %convert_bitcast_fusion), calls=%async_computation | async-start | bytes 3670016 | tf_op jit(solution)/shard_map/all_to_all | solution.py:139
  29.7 1.2 slice.78
  31.5 18.5 %all-gather.3 = s32[16,1,512]{2,1,0:T(1,128)S(1)} all-gather(s32[1,1,512]{2,1,0:T(1,128)S(1)} %bitcast.61), channel_id=2, replica_groups=mesh['z'=8,'x'=4,'y'=8,'core'=2] {'y','core'}, dimensions={0}, use_global_device_ids=true | all-gather | bytes 34816 | tf_op jit(solution)/shard_map/all_gather | solution.py:140
  50.1 0.5 slice.79
  51.2 21.5 %all-to-all-done = f16[32,8,3584]{2,1,0:T(8,128)(2,1)S(1)} async-done(((f16[32,8,3584]{2,1,0:T(8,128)(2,1)}), f16[32,8,3584]{2,1,0:T(8,128)(2,1)S(1)}, u32[]{:S(2)}, u32[]{:S(2)}) %all-to-all-start) | async-done | bytes 1835040 | tf_op jit(solution)/shard_map/all_to_all | solution.py:139
  73.3 0.5 fusion.12
  74.1 0.4 fusion.2
  74.5 0.6 convolution_add_fusion
  75.4 4.4 %collective-permute-start = (f32[8,8,3584]{2,1,0:T(8,128)S(1)}, f32[8,8,3584]{2,1,0:T(8,128)S(1)}, u32[]{:S(2)}, u32[]{:S(2)}) collective-permute-start(f32[8,8,3584]{2,1,0:T(8,128)S(1)} %pad_maximum_fusion), channel_id=1, source_target_pairs={{0,1},{1,0},{2,3},{3,2},{4,5},{5,4},{6,7},{7,6},{8,9},{9,8},{10,11... | collective-permute-start | bytes 2752520 | tf_op jit(solution)/shard_map/ppermute | solution.py:170
  79.8 2.4 %collective-permute-done = f32[8,8,3584]{2,1,0:T(8,128)S(1)} collective-permute-done((f32[8,8,3584]{2,1,0:T(8,128)S(1)}, f32[8,8,3584]{2,1,0:T(8,128)S(1)}, u32[]{:S(2)}, u32[]{:S(2)}) %collective-permute-start) | collective-permute-done | bytes 917536 | tf_op jit(solution)/shard_map/ppermute | solution.py:170
  82.2 1.1 fusion.3
  83.2 6.7 %all-to-all-start.1 = ((f32[8,8,3584]{2,1,0:T(8,128)}), f32[8,8,3584]{2,1,0:T(8,128)S(1)}, u32[]{:S(2)}, u32[]{:S(2)}) async-start(f32[8,8,3584]{2,1,0:T(8,128)} %fusion.3), calls=%async_computation.1 | async-start | bytes 1835008 | tf_op jit(solution)/shard_map/all_to_all | solution.py:171
  89.9 0.4 multiply_reduce_fusion
  90.3 1.0 copy.23.square_ref
  91.5 0.2 multiply_reduce_fusion.1
  91.7 1.2 slice.85
  93.5 0.5 broadcast_add_fusion.4.pick_ref
  94.2 9.9 %shard_map.77 = f32[16,1,512]{2,1,0:T(1,128)} custom-call(s32[16]{0:T(128)} %broadcast_add_fusion.4.pick_ref, bf16[8,128,768]{2,1,0:T(8,128)(2,1)} %cents_ref.1, f32[8,128,1]{2,1,0:T(8,128)} %copy.23.square_ref, bf16[16,512,768]{2,1,0:T(8,128)(2,1)} %bitcast.48), custom_call_target="tpu_custom_call" | custom-call | flops 1610612736 | bytes 12582912 | tf_op jit(solution)/shard_map/pallas_call | solution.py:97
  104.1 0.8 copy.41
  104.9 0.5 slice.86
  106.1 10.2 %all-to-all-done.1 = f32[8,8,3584]{2,1,0:T(8,128)S(1)} async-done(((f32[8,8,3584]{2,1,0:T(8,128)}), f32[8,8,3584]{2,1,0:T(8,128)S(1)}, u32[]{:S(2)}, u32[]{:S(2)}) %all-to-all-start.1) | async-done | bytes 917536 | tf_op jit(solution)/shard_map/all_to_all | solution.py:171
  116.4 0.5 slice.91
  117.6 0.8 broadcast_in_dim.170
  118.4 10.0 %all-to-all-start.2 = ((f32[32,4,896]{2,1,0:T(4,128)}), f32[32,4,896]{2,1,0:T(4,128)S(1)}, u32[]{:S(2)}, u32[]{:S(2)}) async-start(f32[32,4,896]{2,1,0:T(4,128)} %broadcast_in_dim.170), calls=%async_computation.2 | async-start | bytes 917504 | tf_op jit(solution)/shard_map/all_to_all | solution.py:182
  128.5 17.5 %all-gather.2 = f32[256,1,512]{2,1,0:T(1,128)S(1)} all-gather(f32[16,1,512]{2,1,0:T(1,128)S(1)} %bitcast.55), channel_id=4, replica_groups=mesh['z'=8,'x'=4,'y'=8,'core'=2] {'y','core'}, dimensions={0}, use_global_device_ids=true | all-gather | bytes 557056 | tf_op jit(solution)/shard_map/all_gather | solution.py:185
  146.1 0.5 slice.92
  147.3 0.6 add_multiply_fusion
  148.2 0.8 fusion.4
  149.1 1.6 %fusion.5 = f32[8,4,768]{2,1,0:T(4,128)} fusion(f32[8,4,768]{2,0,1:T(8,128)S(1)} %bitcast.53, f32[8,4]{1,0:T(8,128)S(1)} %dynamic-slice_add_fusion, bf16[8,128,768]{2,1,0:T(8,128)(2,1)} %cents_ref.1, s32[]{:T(128)S(6)} %select_n.175), kind=kLoop, calls=%fused_computation.22 | loop fusion | flops 98304 | bytes 245892 | tf_op jit(solution)/shard_map/div | solution.py:195
  (49 shorter events, 2.0 us)
Async XLA Ops:
  7.2 87.0 %all-gather.6.cloned.1.call-start = ((), (), s32[]{:S(2)}) async-start(), calls=%async_computation.3 | async-start | bytes 13369344 | tf_op jit(solution)/shard_map/all_gather | solution.py:135
  15.8 15.7 %copy-start.5 = (s32[512]{0:T(512)S(1)}, s32[512]{0:T(512)}, u32[]{:S(2)}) copy-start(s32[512]{0:T(512)} %param.6) | copy-start | bytes 6148
  15.8 56.9 %all-to-all-start = ((f16[32,8,3584]{2,1,0:T(8,128)(2,1)}), f16[32,8,3584]{2,1,0:T(8,128)(2,1)S(1)}, u32[]{:S(2)}, u32[]{:S(2)}) async-start(f16[32,8,3584]{2,1,0:T(8,128)(2,1)} %convert_bitcast_fusion), calls=%async_computation | async-start | bytes 3670016 | tf_op jit(solution)/shard_map/all_to_all | solution.py:139
  75.4 6.8 %collective-permute-start = (f32[8,8,3584]{2,1,0:T(8,128)S(1)}, f32[8,8,3584]{2,1,0:T(8,128)S(1)}, u32[]{:S(2)}, u32[]{:S(2)}) collective-permute-start(f32[8,8,3584]{2,1,0:T(8,128)S(1)} %pad_maximum_fusion), channel_id=1, source_target_pairs={{0,1},{1,0},{2,3},{3,2},{4,5},{5,4},{6,7},{7,6},{8,9},{9,8},{10,11... | collective-permute-start | bytes 2752520 | tf_op jit(solution)/shard_map/ppermute | solution.py:170
  82.2 7.8 %copy-start.1 = (bf16[8,128,768]{2,1,0:T(8,128)(2,1)S(1)}, bf16[8,128,768]{2,1,0:T(8,128)(2,1)}, u32[]{:S(2)}) copy-start(bf16[8,128,768]{2,1,0:T(8,128)(2,1)} %cents_ref.1) | copy-start | bytes 4718596
  83.2 8.2 %copy-start = (bf16[512,768]{1,0:T(8,128)(2,1)S(1)}, bf16[512,768]{1,0:T(8,128)(2,1)}, u32[]{:S(2)}) copy-start(bf16[512,768]{1,0:T(8,128)(2,1)} %rows_ref.1) | copy-start | bytes 2359300
  83.2 33.1 %all-to-all-start.1 = ((f32[8,8,3584]{2,1,0:T(8,128)}), f32[8,8,3584]{2,1,0:T(8,128)S(1)}, u32[]{:S(2)}, u32[]{:S(2)}) async-start(f32[8,8,3584]{2,1,0:T(8,128)} %fusion.3), calls=%async_computation.1 | async-start | bytes 1835008 | tf_op jit(solution)/shard_map/all_to_all | solution.py:171
  104.1 24.4 %copy-start.4 = (f32[16,1,512]{2,1,0:T(1,128)S(1)}, f32[16,1,512]{2,1,0:T(1,128)}, u32[]{:S(2)}) copy-start(f32[16,1,512]{2,1,0:T(1,128)} %shard_map.77) | copy-start | bytes 98308
  116.4 31.5 %copy-start.2 = (f32[8,3584]{1,0:T(8,128)}, f32[8,3584]{1,0:T(8,128)S(1)}, u32[]{:S(2)}) copy-start(f32[8,3584]{1,0:T(8,128)S(1)} %add_reduce_fusion) | copy-start | bytes 344068
  118.4 29.4 %all-to-all-start.2 = ((f32[32,4,896]{2,1,0:T(4,128)}), f32[32,4,896]{2,1,0:T(4,128)S(1)}, u32[]{:S(2)}, u32[]{:S(2)}) async-start(f32[32,4,896]{2,1,0:T(4,128)} %broadcast_in_dim.170), calls=%async_computation.2 | async-start | bytes 917504 | tf_op jit(solution)/shard_map/all_to_all | solution.py:182
  128.5 19.7 %copy-start.3 = (f32[128,768]{1,0:T(8,128)S(1)}, f32[128,768]{1,0:T(8,128)}, u32[]{:S(2)}) copy-start(f32[128,768]{1,0:T(8,128)} %param.8) | copy-start | bytes 1179652
  147.9 1.2 slice-start
Sparse Core Ops, SparseCore 0:
  10.1 84.0 all-gather.5

commit v5 on v4

v5 whole, which is shorter than its diff:
```python
import functools

import jax
import jax.numpy as jnp
from jax import lax
from jax.experimental import pallas as pl
from jax.experimental.pallas import tpu as pltpu
from jax.sharding import Mesh, PartitionSpec as P

COARSE = 128
DP = ("z", "x")
CENT = ("y", "core")
STEPS = 13
VMEM = 56 * 2**20


def message_kernel(share, owned, coarse_ref, fine_ref, rows_ref, out_ref):
    count, width = rows_ref.shape
    per = 128
    lines = out_ref.shape[0]
    slots = 8
    coarse = coarse_ref[...]
    local = fine_ref[...] - coarse * per
    owner = coarse // owned

    owners = lax.broadcasted_iota(jnp.int32, (16, count), 0)
    present = jnp.max((owners == owner).astype(jnp.int32), axis=1, keepdims=True)
    slot_row = jnp.sum(jnp.where(owners < owner, present, 0), axis=0, keepdims=True)
    slot_ids = lax.broadcasted_iota(jnp.int32, (slots, count), 0)
    cluster = jnp.max(jnp.where(slot_ids == slot_row, coarse, 0), axis=1, keepdims=True)

    largest = jnp.max(jnp.abs(rows_ref[...]).astype(jnp.float32))
    scale, step = 1.0, 0.0
    for k in range(1, STEPS):
        fits = largest * 256.0**k <= 60000.0 / count
        scale = jnp.where(fits, 256.0**k, scale)
        step = jnp.where(fits, float(k), step)

    line = lax.broadcasted_iota(jnp.int32, (lines, 1), 0)
    key = slot_row * per + local
    target = (line % slots) * per + (line // slots) * share
    lane = lax.broadcasted_iota(jnp.int32, (lines, per), 1) % (per // 2)
    ones = jnp.ones((count, per), jnp.bfloat16)
    notes = jnp.broadcast_to(step, (lines, per))
    for j in range(share):
        hot = (target + j == key).astype(jnp.bfloat16)
        part = jnp.dot(hot, rows_ref[...], preferred_element_type=jnp.float32)
        out_ref[:, j * width : (j + 1) * width] = part * scale
        notes = jnp.where(lane == j, jnp.dot(hot, ones, preferred_element_type=jnp.float32), notes)
    hot = (slot_ids == slot_row).astype(jnp.bfloat16)
    part = jnp.dot(hot, rows_ref[...], preferred_element_type=jnp.float32) * scale
    number = jnp.dot(hot, ones, preferred_element_type=jnp.float32)
    cluster = jnp.broadcast_to(cluster.astype(jnp.float32), (slots, per))

    def spread(piece):
        whole = jnp.broadcast_to(piece[None], (lines // slots,) + piece.shape)
        return whole.reshape(lines, piece.shape[1])

    notes = jnp.where(lane == share, spread(number), jnp.where(lane == share + 1, spread(cluster), notes))
    out_ref[:, share * width : (share + 1) * width] = spread(part)
    out_ref[:, (share + 1) * width :] = notes


def message_of(coarse_ids, fine_ids, rows, planes, share, owned):
    width = rows.shape[1]
    shape = (planes * 8, (share + 1) * width + 128)
    return pl.pallas_call(
        functools.partial(message_kernel, share, owned),
        in_specs=[pl.BlockSpec(memory_space=pltpu.VMEM)] * 3,
        out_specs=pl.BlockSpec(memory_space=pltpu.VMEM),
        out_shape=jax.ShapeDtypeStruct(shape, jnp.float32),
        compiler_params=pltpu.CompilerParams(vmem_limit_bytes=VMEM),
        cost_estimate=pl.CostEstimate(
            flops=2 * shape[0] * shape[1] * rows.shape[0], bytes_accessed=16 * rows.size, transcendentals=0
        ),
    )(coarse_ids[None, :], fine_ids[None, :], rows)


def gaps_kernel(pick_ref, cents_ref, square_ref, rows_ref, out_ref, held, sems):
    sources = rows_ref.shape[0]

    def fetch(s):
        return pltpu.make_async_copy(rows_ref.at[s], held.at[s], sems.at[s])

    for s in range(sources):
        fetch(s).start()

    @pl.loop(0, sources, unroll=4)
    def _(s):
        c = pick_ref[s]
        fetch(s).wait()
        dots = lax.dot_general(
            cents_ref[c], held[s], (((1,), (1,)), ((), ())), preferred_element_type=jnp.float32
        )
        out_ref[s] = jnp.min(square_ref[c] - 2.0 * dots, axis=0, keepdims=True)


def nearest(pick, cents, squares, rows):
    sources, per_source, width = rows.shape
    return pl.pallas_call(
        gaps_kernel,
        in_specs=[
            pl.BlockSpec(memory_space=pltpu.SMEM),
            pl.BlockSpec(memory_space=pltpu.VMEM),
            pl.BlockSpec(memory_space=pltpu.VMEM),
            pl.BlockSpec(memory_space=pl.ANY),
        ],
        out_specs=pl.BlockSpec(memory_space=pltpu.VMEM),
        out_shape=jax.ShapeDtypeStruct((sources, 1, per_source), jnp.float32),
        scratch_shapes=[
            pltpu.VMEM(rows.shape, rows.dtype),
            pltpu.SemaphoreType.DMA((sources,)),
        ],
        compiler_params=pltpu.CompilerParams(vmem_limit_bytes=VMEM),
        cost_estimate=pl.CostEstimate(
            flops=2 * cents.shape[1] * rows.size, bytes_accessed=2 * rows.size, transcendentals=0
        ),
    )(pick, cents, squares, rows)


def settle_kernel(per, anchors, arrived_ref, fine_ref, coarse_ref, least_ref, new_fine_ref, news_ref):
    blocks, lines, columns = arrived_ref.shape
    wide = columns - per
    width = coarse_ref.shape[1]
    share = wide // width - 1
    factors = []
    notes = jnp.zeros((lines, per), jnp.float32)
    for y in range(blocks):
        step = arrived_ref[y, :1, wide:][:, per - 1 :]
        factor = jnp.full_like(step, 16.0)
        for k in range(1, STEPS):
            factor = jnp.where(step == k, 16.0 * 256.0**-k, factor)
        factors.append(factor)
        notes += arrived_ref[y, :, wide:]

    def total(j):
        at = pl.ds(j * width, width)
        found = arrived_ref[0, :, at] * factors[0]
        for y in range(1, blocks):
            found += arrived_ref[y, :, at] * factors[y]
        number = 64.0 * notes[:, j : j + 1] + notes[:, per // 2 + j : per // 2 + j + 1]
        return found, number

    found, number = total(share)
    ours = (anchors[0] * coarse_ref[...] + found) / (anchors[0] + number)
    sources, count = least_ref.shape
    half = lines // 2
    news_ref[:sources] = least_ref[...]
    news_ref[sources : sources + lines] = ours[:, :count]
    news_ref[sources + lines :] = jnp.concatenate([ours[:half, count:], ours[half:, count:]], axis=1)
    for j in range(share):
        found, number = total(j)
        new_fine_ref[:, j, :] = (anchors[1] * fine_ref[:, pl.ds(j * width, width)] + found) / (anchors[1] + number)


def settle(arrived, fine, coarse, least, per, anchors):
    lines, width = coarse.shape
    sources, count = least.shape
    return pl.pallas_call(
        functools.partial(settle_kernel, per, anchors),
        in_specs=[pl.BlockSpec(memory_space=pltpu.VMEM)] * 4,
        out_specs=[pl.BlockSpec(memory_space=pltpu.VMEM)] * 2,
        out_shape=[
            jax.ShapeDtypeStruct((lines, fine.shape[1] // width, width), jnp.float32),
            jax.ShapeDtypeStruct((sources + lines + lines // 2, count), jnp.float32),
        ],
        compiler_params=pltpu.CompilerParams(vmem_limit_bytes=VMEM),
    )(arrived, fine, coarse, least)


def after(value, earlier):
    return value + (earlier[(0,) * earlier.ndim].astype(jnp.float32) * 0.0).astype(value.dtype)


def power(step):
    up, down = jnp.ones_like(step), jnp.ones_like(step)
    for k in range(1, STEPS):
        up = jnp.where(step == k, 256.0**k, up)
        down = jnp.where(step == k, 256.0**-k, down)
    return up, down


def join_kernel(per, kept_ref, got_ref, out_ref):
    blocks, lines, columns = kept_ref.shape
    wide = columns - per
    lane = lax.broadcasted_iota(jnp.int32, (lines, per), 1)
    step = jnp.minimum(kept_ref[0, :1, wide:], got_ref[0, :1, wide:])[:, per - 1 :]
    scale = power(step)[0] * 0.0625
    for y in range(blocks):
        out_ref[y, :, :wide] = (kept_ref[y, :, :wide] + got_ref[y, :, :wide]) * scale
        notes = kept_ref[y, :, wide:] + got_ref[y, :, wide:]
        high = jnp.floor(notes * (1.0 / 64.0))
        notes = jnp.where(lane < per // 2, high, notes - 64.0 * high)
        out_ref[y, :, wide:] = jnp.where(lane == per - 1, jnp.broadcast_to(step, notes.shape), notes)


def join(kept, got, per):
    return pl.pallas_call(
        functools.partial(join_kernel, per),
        in_specs=[pl.BlockSpec(memory_space=pltpu.VMEM)] * 2,
        out_specs=pl.BlockSpec(memory_space=pltpu.VMEM),
        out_shape=jax.ShapeDtypeStruct(kept.shape, jnp.float32),
        compiler_params=pltpu.CompilerParams(vmem_limit_bytes=VMEM),
    )(kept, got)


def body(embeds, coarse_ids, fine_ids, coarse_cents, fine_cents):
    blk, per, width = fine_cents.shape
    count = embeds.shape[0]
    planes = lax.axis_size(DP)
    owners = lax.axis_size(CENT)
    share = per // planes
    slots = 8
    me = lax.axis_index(CENT)
    core = lax.axis_index("core")
    anchor_coarse = count * planes * owners // COARSE
    anchor_fine = max(1, anchor_coarse // per)

    rows = lax.all_gather(embeds, CENT, axis=0, tiled=False)

    message = message_of(coarse_ids, fine_ids, embeds, planes, share, blk)
    heard = message.astype(jnp.float16).reshape(planes, slots, -1)
    heard = lax.all_to_all(heard, DP, split_axis=0, concat_axis=0, tiled=True)
    sent = lax.all_gather(after(coarse_ids, message), CENT, axis=0, tiled=False)

    near = sent - me * blk
    pick = jnp.max(jnp.where((near >= 0) & (near < blk), near, 0), axis=1)
    squares = jnp.sum(jnp.square(fine_cents.astype(jnp.float32)), axis=2, keepdims=True)
    first = lax.axis_index(DP) * share
    fine = lax.dynamic_slice_in_dim(fine_cents, first, share, 1).astype(jnp.float32).reshape(blk, share * width)
    coarse = lax.dynamic_slice_in_dim(coarse_cents, me * blk, blk, 0)
    wide = (share + 1) * width
    notes = heard[:, :, wide:].astype(jnp.float32)
    for ready in (pick, squares, fine, coarse):
        notes = after(notes, ready)
    step = notes[:, 0, per - 1]
    found = jnp.arange(COARSE, dtype=jnp.float32)[:, None, None] == notes[None, :, :, share + 1]
    weights = jnp.where(found, jnp.exp2(-8.0 * step)[None, :, None], 0.0)
    weights = weights.reshape(COARSE, planes * slots).astype(jnp.bfloat16)
    values = heard[:, :, :wide].reshape(planes * slots, wide).astype(jnp.float32)
    high = lax.reduce_precision(values, 8, 7)
    low = (values - high).astype(jnp.bfloat16)
    table = jnp.dot(weights, high.astype(jnp.bfloat16), preferred_element_type=jnp.float32)
    table = table + jnp.dot(weights, low, preferred_element_type=jnp.float32)
    plain = found.reshape(COARSE, planes * slots).astype(jnp.bfloat16)
    notes = notes.reshape(planes * slots, per).astype(jnp.bfloat16)
    notes = jnp.dot(plain, notes, preferred_element_type=jnp.float32)
    notes = jnp.where(jnp.arange(per, dtype=jnp.int32)[None, :] == per - 1, jnp.min(step), notes)

    table = jnp.concatenate([table, notes], axis=1).reshape(owners // 2, 2, blk, wide + per)
    kept = lax.dynamic_index_in_dim(table, core, 1, keepdims=False)
    given = lax.dynamic_index_in_dim(table, 1 - core, 1, keepdims=False)
    got = lax.ppermute(given, "core", [(0, 1), (1, 0)])
    both = join(kept, got, per).astype(jnp.float16)
    arrived = lax.all_to_all(both, "y", split_axis=0, concat_axis=0, tiled=True)
    least = nearest(after(pick, both), fine_cents, squares, rows)[:, 0]
    arrived = after(arrived.astype(jnp.float32), least)
    anchors = (float(anchor_coarse), float(anchor_fine))
    new_fine, news = settle(arrived, fine, coarse, least, per, anchors)

    news = lax.all_gather(news, CENT, axis=0, tiled=False)
    tails = news[:, owners + blk :]
    tails = jnp.concatenate([tails[:, :, : width - count], tails[:, :, width - count :]], axis=1)
    new_coarse = jnp.concatenate([news[:, owners : owners + blk], tails], axis=2).reshape(COARSE, width)
    back = lax.dynamic_index_in_dim(news, me, 1, keepdims=False)
    row_sq = jnp.sum(jnp.square(embeds.astype(jnp.float32)), axis=1)
    at = (coarse_ids // blk)[None, :] == jnp.arange(owners, dtype=jnp.int32)[:, None]
    gaps = (row_sq + jnp.sum(jnp.where(at, back, 0.0), axis=0)) / width
    return (new_fine, new_coarse, gaps)


def solution(mesh):
    fine_mesh = Mesh(mesh.devices.reshape(8, 4, 8, 2), DP + CENT)
    placed = (P(DP + CENT, None), P(DP + CENT), P(DP + CENT), P(), P(CENT, None, None))
    return jax.shard_map(
        body,
        mesh=fine_mesh,
        in_specs=placed,
        out_specs=(P(CENT, DP, None), P(), P(DP + CENT)),
        check_vma=False,
    )
```

time: 158 us -> 152 us (0.962)
  waiting for transfers between devices: 34.9 us -> 24.8 us
  starting transfers between devices: 35 us -> 25.3 us
  Pallas kernels: 14.3 us -> 19.4 us
  other arithmetic: 9.93 us -> 15 us
  blocking collectives: 36 us -> 37.7 us
  matrix products: 1.01 us -> 2.65 us
    all_to_all x1 -> x0, starting transfers between devices: 10 us -> none  [body(): lax.all_to_all(jnp.broadcast_to(mine[None], (planes,) + mine.shape), DP,...]
    all_to_all x1, waiting for transfers between devices: 10.2 us -> 1.79 us  [body(): arrived = lax.all_to_all(both, 'y', split_axis=0, concat_axis=0, tiled=True)]
    pallas_call x0 -> x2, Pallas kernels: none -> 4.82 us  [the longest x1 2.71 us: join(): pl.pallas_call(functools.partial(join_kernel, per), in_specs=[pl.BlockSpe...]
    div x2 -> x0, other arithmetic: 2.47 us -> none  [the longest x1 1.62 us: body(): (anchor_fine * former + fine_sum) / (anchor_fine + fine_num[:, :, None])]
    convert_element_type x1, other arithmetic: 0.01 us -> 2.13 us  [body(): both = join(kept, got, per).astype(jnp.float16)]
    add x4 -> x3, other arithmetic: 0.58 us -> 2.29 us  [after(): value + (earlier[(0,) * earlier.ndim].astype(jnp.float32) * 0.0).astype(v...]
    all_gather x1, blocking collectives: 17.5 us -> 19.2 us  [body(): news = lax.all_gather(news, CENT, axis=0, tiled=False)]
    dot_general x2 -> x3, matrix products: 1.01 us -> 2.65 us  [the longest x1 1.43 us: body(): notes = jnp.dot(plain, notes, preferred_element_type=jnp.float32)]
  transfers between devices with their start and end apart: 5 -> 4, of which waited for: 4 -> 3; matrix products, arithmetic and copies ran while one was open for 9% -> 15% of each run, Pallas kernels for 9% -> 11%
where the time goes in v5:
time: 152 us; the launch traced here: 151 us
  blocking collectives  37.7 us (25%)
  starting transfers between devices  25.3 us (17%)
  waiting for transfers between devices  24.8 us (16%)
  Pallas kernels  19.4 us (13%)
  between operations  17.4 us (11%)
  other arithmetic  15 us (10%)
  local copies, waits for them, and re-layouts  8.91 us (6%)
  matrix products  2.65 us (2%)
    all_to_all x1, waiting for transfers between devices, body(): heard = lax.all_to_all(heard, DP, split_axis=0, concat_axis=0, tiled=True)  20.1 us
    all_gather x1, blocking collectives, body(): news = lax.all_gather(news, CENT, axis=0, tiled=False)  19.2 us
    all_gather x1, blocking collectives, body(): sent = lax.all_gather(after(coarse_ids, message), CENT, axis=0, tiled=False)  18.5 us
    all_to_all x1, starting transfers between devices, body(): heard = lax.all_to_all(heard, DP, split_axis=0, concat_axis=0, tiled=True)  13.8 us
    pallas_call x1, Pallas kernels, nearest(): pl.pallas_call(gaps_kernel, in_specs=[pl.BlockSpec(memory_space=pltpu.SME...  9.89 us
    all_to_all x1, starting transfers between devices, body(): arrived = lax.all_to_all(both, 'y', split_axis=0, concat_axis=0, tiled=True)  6.98 us
    pallas_call x1, Pallas kernels, message_of(): pl.pallas_call(functools.partial(message_kernel, share, owned), in_specs=...  4.65 us
    ppermute x1, starting transfers between devices, body(): got = lax.ppermute(given, 'core', [(0, 1), (1, 0)])  4.45 us
  transfers between devices with their start and end apart: 4, of which 3 were waited for; matrix products, arithmetic and copies ran while one was open for 15% of the time, Pallas kernels for 11%

profile of v5, /device:TPU:1, one launch (start us, length us, event | category | flops | bytes accessed | tf_op | source)
XLA Modules:
  0.0 151.1 jit_solution(5609949380565437303)
XLA Ops:
  7.2 0.7 all-gather.7.cloned.1.call-update
  7.9 4.6 %shard_map.76 = f32[256,3968]{1,0:T(8,128)} custom-call(s32[1,512]{1,0:T(1,128)} %bitcast.73, s32[1,512]{1,0:T(1,128)} %bitcast.75, bf16[512,768]{1,0:T(8,128)(2,1)} %rows_ref.1), custom_call_target="tpu_custom_call" | custom-call | flops 1040187392 | bytes 6291456 | tf_op jit(solution)/shard_map/pallas_call | solution.py:67
  12.5 3.7 %convert_bitcast_fusion = f16[32,8,3968]{2,1,0:T(8,128)(2,1)} fusion(f32[256,3968]{1,0:T(8,128)} %shard_map.76), kind=kLoop, calls=%fused_computation.6 | loop fusion | flops 1015808 | bytes 6094848 | tf_op jit(solution)/shard_map/reshape | solution.py:222
  16.2 13.8 %all-to-all-start = ((f16[32,8,3968]{2,1,0:T(8,128)(2,1)}), f16[32,8,3968]{2,1,0:T(8,128)(2,1)S(1)}, u32[]{:S(2)}, u32[]{:S(2)}) async-start(f16[32,8,3968]{2,1,0:T(8,128)(2,1)} %convert_bitcast_fusion), calls=%async_computation | async-start | bytes 4063232 | tf_op jit(solution)/shard_map/all_to_all | solution.py:223
  30.1 1.2 slice.60
  31.3 0.9 convert_bitcast_fusion.1
  34.0 18.5 %all-gather.3 = s32[16,1,512]{2,1,0:T(1,128)S(1)} all-gather(s32[1,1,512]{2,1,0:T(1,128)S(1)} %bitcast.74), channel_id=2, replica_groups=mesh['z'=8,'x'=4,'y'=8,'core'=2] {'y','core'}, dimensions={0}, use_global_device_ids=true | all-gather | bytes 34816 | tf_op jit(solution)/shard_map/all_gather | solution.py:224
  52.7 1.8 %multiply_reduce_fusion = f32[8,128]{1,0:T(8,128)S(1)} fusion(bf16[8,128,768]{2,1,0:T(8,128)(2,1)} %cents_ref.1), kind=kLoop, calls=%fused_computation.4 | loop fusion | flops 2358272 | bytes 1576960 | tf_op jit(solution)/shard_map/reduce_sum | solution.py:228
  54.7 0.6 slice.61
  55.3 1.2 fusion.20
  57.1 20.1 %all-to-all-done = f16[32,8,3968]{2,1,0:T(8,128)(2,1)S(1)} async-done(((f16[32,8,3968]{2,1,0:T(8,128)(2,1)}), f16[32,8,3968]{2,1,0:T(8,128)(2,1)S(1)}, u32[]{:S(2)}, u32[]{:S(2)}) %all-to-all-start) | async-done | bytes 2031648 | tf_op jit(solution)/shard_map/all_to_all | solution.py:223
  77.2 0.7 add_add_fusion
  78.2 1.0 exponential_reduce_fusion
  79.4 1.4 convolution_select_fusion
  81.3 0.8 convolution_add_fusion
  82.2 1.1 dynamic-slice_bitcast_fusion
  83.3 4.5 %collective-permute-start = (f32[8,8,3968]{2,1,0:T(8,128)S(1)}, f32[8,8,3968]{2,1,0:T(8,128)S(1)}, u32[]{:S(2)}, u32[]{:S(2)}) collective-permute-start(f32[8,8,3968]{2,1,0:T(8,128)S(1)} %get-tuple-element.9), channel_id=1, source_target_pairs={{0,1},{1,0},{2,3},{3,2},{4,5},{5,4},{6,7},{7,6},{8,9},{9,8},{10,11... | collective-permute-start | bytes 3047432 | tf_op jit(solution)/shard_map/ppermute | solution.py:253
  87.8 2.2 %collective-permute-done.got_ref = f32[8,8,3968]{2,1,0:T(8,128)S(1)} collective-permute-done((f32[8,8,3968]{2,1,0:T(8,128)S(1)}, f32[8,8,3968]{2,1,0:T(8,128)S(1)}, u32[]{:S(2)}, u32[]{:S(2)}) %collective-permute-start) | collective-permute-done | bytes 1015840 | tf_op jit(solution)/shard_map/ppermute | solution.py:253
  90.0 1.0 copy-done.2
  91.0 2.7 %shard_map.77 = f32[8,8,3968]{2,1,0:T(8,128)} custom-call(f32[8,8,3968]{2,1,0:T(8,128)} %get-tuple-element.10.kept_ref, f32[8,8,3968]{2,1,0:T(8,128)} %copy-done.2), custom_call_target="tpu_custom_call" | custom-call | tf_op jit(solution)/shard_map/pallas_call | solution.py:198
  93.7 2.1 %convert_element_type.74 = f16[8,8,3968]{2,1,0:T(8,128)(2,1)} convert(f32[8,8,3968]{2,1,0:T(8,128)} %shard_map.77) | non-fusion elementwise | flops 253952 | bytes 1523712 | tf_op jit(solution)/shard_map/convert_element_type | solution.py:254
  95.8 7.0 %all-to-all-start.1 = ((f16[8,8,3968]{2,1,0:T(8,128)(2,1)}), f16[8,8,3968]{2,1,0:T(8,128)(2,1)S(1)}, u32[]{:S(2)}, u32[]{:S(2)}) async-start(f16[8,8,3968]{2,1,0:T(8,128)(2,1)} %convert_element_type.74), calls=%async_computation.1 | async-start | bytes 1015808 | tf_op jit(solution)/shard_map/all_to_all | solution.py:255
  102.8 1.3 constant_dynamic-slice_fusion.2.coarse_ref
  104.4 1.2 slice.66
  106.8 9.9 %shard_map.78 = f32[16,1,512]{2,1,0:T(1,128)} custom-call(s32[16]{0:T(128)} %broadcast_add_fusion.1.pick_ref, bf16[8,128,768]{2,1,0:T(8,128)(2,1)} %cents_ref.1, f32[8,128,1]{2,1,0:T(8,128)} %copy-done.1, bf16[16,512,768]{2,1,0:T(8,128)(2,1)} %bitcast.63), custom_call_target="tpu_custom_call" | custom-call | flops 1610612736 | bytes 12582912 | tf_op jit(solution)/shard_map/pallas_call | solution.py:100
  116.7 0.8 copy.37
  118.6 1.8 %all-to-all-done.1 = f16[8,8,3968]{2,1,0:T(8,128)(2,1)S(1)} async-done(((f16[8,8,3968]{2,1,0:T(8,128)(2,1)}), f16[8,8,3968]{2,1,0:T(8,128)(2,1)S(1)}, u32[]{:S(2)}, u32[]{:S(2)}) %all-to-all-start.1) | async-done | bytes 507936 | tf_op jit(solution)/shard_map/all_to_all | solution.py:255
  120.4 1.0 convert_add_fusion.arrived_ref
  121.4 2.1 %shard_map.79 = (f32[8,4,768]{2,1,0:T(4,128)}, f32[28,512]{1,0:T(8,128)}) custom-call(f32[8,8,3968]{2,1,0:T(8,128)} %convert_add_fusion.arrived_ref, f32[8,3072]{1,0:T(8,128)} %bitcast.66, f32[8,768]{1,0:T(8,128)} %constant_dynamic-slice_fusion.2.coarse_ref, f32[16,512]{1,0:T(8,128)} %bitcast.68), custom_call_target="tpu_custom_call" | custom-call | tf_op jit(solution)/shard_map/pallas_call | solution.py:159
  123.6 19.2 %all-gather.4 = f32[16,28,512]{2,1,0:T(8,128)S(1)} all-gather(f32[1,28,512]{2,1,0:T(8,128)} %bitcast.71), channel_id=4, replica_groups=mesh['z'=8,'x'=4,'y'=8,'core'=2] {'y','core'}, dimensions={0}, use_global_device_ids=true | all-gather | bytes 974848 | tf_op jit(solution)/shard_map/all_gather | solution.py:261
  142.8 0.6 add_multiply_fusion
  143.4 0.8 maximum_bitcast_fusion
  (33 shorter events, 3.4 us)
Async XLA Ops:
  7.2 99.6 %all-gather.7.cloned.1.call-start = ((), (), s32[]{:S(2)}) async-start(), calls=%async_computation.2 | async-start | bytes 13369344 | tf_op jit(solution)/shard_map/all_gather | solution.py:219
  16.2 17.7 %copy-start.5 = (s32[512]{0:T(512)S(1)}, s32[512]{0:T(512)}, u32[]{:S(2)}) copy-start(s32[512]{0:T(512)} %param.6) | copy-start | bytes 6148
  16.2 61.0 %all-to-all-start = ((f16[32,8,3968]{2,1,0:T(8,128)(2,1)}), f16[32,8,3968]{2,1,0:T(8,128)(2,1)S(1)}, u32[]{:S(2)}, u32[]{:S(2)}) async-start(f16[32,8,3968]{2,1,0:T(8,128)(2,1)} %convert_bitcast_fusion), calls=%async_computation | async-start | bytes 4063232 | tf_op jit(solution)/shard_map/all_to_all | solution.py:223
  32.2 49.1 %copy-start.3 = (f32[1,8,4,768]{3,1,2,0:T(8,128)}, f32[1,8,4,768]{3,1,2,0:T(8,128)S(1)}, u32[]{:S(2)}) copy-start(f32[1,8,4,768]{3,1,2,0:T(8,128)S(1)} %copy.33) | copy-start | bytes 294916
  54.7 26.6 %copy-start.1 = (f32[8,128,1]{2,1,0:T(8,128)}, f32[8,128,1]{2,1,0:T(8,128)S(1)}, u32[]{:S(2)}) copy-start(f32[8,128,1]{2,1,0:T(8,128)S(1)} %copy.22.square_ref) | copy-start | bytes 12292
  83.3 6.7 %collective-permute-start = (f32[8,8,3968]{2,1,0:T(8,128)S(1)}, f32[8,8,3968]{2,1,0:T(8,128)S(1)}, u32[]{:S(2)}, u32[]{:S(2)}) collective-permute-start(f32[8,8,3968]{2,1,0:T(8,128)S(1)} %get-tuple-element.9), channel_id=1, source_target_pairs={{0,1},{1,0},{2,3},{3,2},{4,5},{5,4},{6,7},{7,6},{8,9},{9,8},{10,11... | collective-permute-start | bytes 3047432 | tf_op jit(solution)/shard_map/ppermute | solution.py:253
  90.0 1.0 copy-start.2
  93.7 10.5 %copy-start = (bf16[512,768]{1,0:T(8,128)(2,1)S(1)}, bf16[512,768]{1,0:T(8,128)(2,1)}, u32[]{:S(2)}) copy-start(bf16[512,768]{1,0:T(8,128)(2,1)} %rows_ref.1) | copy-start | bytes 2359300
  95.8 24.6 %all-to-all-start.1 = ((f16[8,8,3968]{2,1,0:T(8,128)(2,1)}), f16[8,8,3968]{2,1,0:T(8,128)(2,1)S(1)}, u32[]{:S(2)}, u32[]{:S(2)}) async-start(f16[8,8,3968]{2,1,0:T(8,128)(2,1)} %convert_element_type.74), calls=%async_computation.1 | async-start | bytes 1015808 | tf_op jit(solution)/shard_map/all_to_all | solution.py:255
  117.4 4.0 %copy-start.4 = (f32[16,1,512]{2,0,1:T(8,128)}, f32[16,1,512]{2,0,1:T(8,128)S(1)}, u32[]{:S(2)}) copy-start(f32[16,1,512]{2,0,1:T(8,128)S(1)} %copy.37) | copy-start | bytes 98308
Sparse Core Ops, SparseCore 0:
  10.1 84.0 all-gather.6

commit v6 on v5

--- a/solution.py
+++ b/solution.py
@@ -11,7 +11,8 @@
 DP = ("z", "x")
 CENT = ("y", "core")
 STEPS = 13
-VMEM = 56 * 2**20
+SMALL = 16 * 2**20
+LARGE = 56 * 2**20
 
 
 def message_kernel(share, owned, coarse_ref, fine_ref, rows_ref, out_ref):
@@ -69,7 +70,7 @@
         in_specs=[pl.BlockSpec(memory_space=pltpu.VMEM)] * 3,
         out_specs=pl.BlockSpec(memory_space=pltpu.VMEM),
         out_shape=jax.ShapeDtypeStruct(shape, jnp.float32),
-        compiler_params=pltpu.CompilerParams(vmem_limit_bytes=VMEM),
+        compiler_params=pltpu.CompilerParams(vmem_limit_bytes=SMALL),
         cost_estimate=pl.CostEstimate(
             flops=2 * shape[0] * shape[1] * rows.shape[0], bytes_accessed=16 * rows.size, transcendentals=0
         ),
@@ -111,7 +112,7 @@
             pltpu.VMEM(rows.shape, rows.dtype),
             pltpu.SemaphoreType.DMA((sources,)),
         ],
-        compiler_params=pltpu.CompilerParams(vmem_limit_bytes=VMEM),
+        compiler_params=pltpu.CompilerParams(vmem_limit_bytes=LARGE),
         cost_estimate=pl.CostEstimate(
             flops=2 * cents.shape[1] * rows.size, bytes_accessed=2 * rows.size, transcendentals=0
         ),
@@ -164,7 +165,7 @@
             jax.ShapeDtypeStruct((lines, fine.shape[1] // width, width), jnp.float32),
             jax.ShapeDtypeStruct((sources + lines + lines // 2, count), jnp.float32),
         ],
-        compiler_params=pltpu.CompilerParams(vmem_limit_bytes=VMEM),
+        compiler_params=pltpu.CompilerParams(vmem_limit_bytes=SMALL),
     )(arrived, fine, coarse, least)
 
 
@@ -200,7 +201,7 @@
         in_specs=[pl.BlockSpec(memory_space=pltpu.VMEM)] * 2,
         out_specs=pl.BlockSpec(memory_space=pltpu.VMEM),
         out_shape=jax.ShapeDtypeStruct(kept.shape, jnp.float32),
-        compiler_params=pltpu.CompilerParams(vmem_limit_bytes=VMEM),
+        compiler_params=pltpu.CompilerParams(vmem_limit_bytes=SMALL),
     )(kept, got)
 
 

time: 152 us -> 142 us (0.934)
  Pallas kernels: 19.4 us -> 12.5 us
  other arithmetic: 15 us -> 10.5 us
  local copies, waits for them, and re-layouts: 8.91 us -> 10.7 us
    unnamed x14 -> x16, local copies, waits for them, and re-layouts: 1.77 us -> 5.19 us
    pallas_call x1, Pallas kernels: 4.65 us -> 1.57 us  [message_of(): pl.pallas_call(functools.partial(message_kernel, share, owned), in_specs=...]
    pallas_call x1, Pallas kernels: 2.71 us -> 0.17 us  [join(): pl.pallas_call(functools.partial(join_kernel, per), in_specs=[pl.BlockSpe...]
    reshape x1, other arithmetic: 3.68 us -> 1.53 us  [body(): heard = message.astype(jnp.float16).reshape(planes, slots, -1)]
  transfers between devices with their start and end apart: 4 -> 4, of which waited for: 3 -> 3; matrix products, arithmetic and copies ran while one was open for 15% -> 13% of each run, Pallas kernels for 11% -> 8%
where the time goes in v6:
time: 142 us; the launch traced here: 141 us
  blocking collectives  36.8 us (26%)
  waiting for transfers between devices  25.4 us (18%)
  starting transfers between devices  25.2 us (18%)
  between operations  17.5 us (12%)
  Pallas kernels  12.5 us (9%)
  local copies, waits for them, and re-layouts  10.7 us (8%)
  other arithmetic  10.5 us (7%)
  matrix products  2.62 us (2%)
    all_to_all x1, waiting for transfers between devices, body(): heard = lax.all_to_all(heard, DP, split_axis=0, concat_axis=0, tiled=True)  20 us
    all_gather x1, blocking collectives, body(): sent = lax.all_gather(after(coarse_ids, message), CENT, axis=0, tiled=False)  18.5 us
    all_gather x1, blocking collectives, body(): news = lax.all_gather(news, CENT, axis=0, tiled=False)  18.3 us
    all_to_all x1, starting transfers between devices, body(): heard = lax.all_to_all(heard, DP, split_axis=0, concat_axis=0, tiled=True)  13.8 us
    pallas_call x1, Pallas kernels, nearest(): pl.pallas_call(gaps_kernel, in_specs=[pl.BlockSpec(memory_space=pltpu.SME...  9.88 us
    all_to_all x1, starting transfers between devices, body(): arrived = lax.all_to_all(both, 'y', split_axis=0, concat_axis=0, tiled=True)  6.79 us
    unnamed x16, local copies, waits for them, and re-layouts  5.19 us
    ppermute x1, starting transfers between devices, body(): got = lax.ppermute(given, 'core', [(0, 1), (1, 0)])  4.5 us
  transfers between devices with their start and end apart: 4, of which 3 were waited for; matrix products, arithmetic and copies ran while one was open for 13% of the time, Pallas kernels for 8%

profile of v6, /device:TPU:1, one launch (start us, length us, event | category | flops | bytes accessed | tf_op | source)
XLA Modules:
  0.0 141.2 jit_solution(15893462389808176159)
XLA Ops:
  7.2 0.7 all-gather.7.cloned.1.call-update
  7.9 1.1 copy-done.1
  9.0 0.7 copy-done.3
  9.7 0.7 copy-done.5
  10.4 1.6 %shard_map.76 = f32[256,3968]{1,0:T(8,128)S(1)} custom-call(s32[1,512]{1,0:T(1,128)S(1)} %bitcast.68, s32[1,512]{1,0:T(1,128)S(1)} %bitcast.69, bf16[512,768]{1,0:T(8,128)(2,1)S(1)} %copy-done.1), custom_call_target="tpu_custom_call" | custom-call | flops 1040187392 | bytes 6291456 | tf_op jit(solution)/shard_map/pallas_call | solution.py:68
  12.0 1.9 %copy-done = f32[256,3968]{1,0:T(8,128)} copy-done((f32[256,3968]{1,0:T(8,128)}, f32[256,3968]{1,0:T(8,128)S(1)}, u32[]{:S(2)}) %copy-start) | copy-done | bytes 4063256
  13.9 1.5 %convert_bitcast_fusion = f16[32,8,3968]{2,1,0:T(8,128)(2,1)} fusion(f32[256,3968]{1,0:T(8,128)S(1)} %shard_map.76), kind=kLoop, calls=%fused_computation.6 | loop fusion | flops 1015808 | bytes 6094848 | tf_op jit(solution)/shard_map/reshape | solution.py:223
  15.4 13.8 %all-to-all-start = ((f16[32,8,3968]{2,1,0:T(8,128)(2,1)}), f16[32,8,3968]{2,1,0:T(8,128)(2,1)S(1)}, u32[]{:S(2)}, u32[]{:S(2)}) async-start(f16[32,8,3968]{2,1,0:T(8,128)(2,1)} %convert_bitcast_fusion), calls=%async_computation | async-start | bytes 4063232 | tf_op jit(solution)/shard_map/all_to_all | solution.py:224
  29.3 1.2 slice.60
  30.5 0.9 convert_bitcast_fusion.1
  33.3 18.5 %all-gather.3 = s32[16,1,512]{2,1,0:T(1,128)S(1)} all-gather(s32[1,1,512]{2,1,0:T(1,128)S(1)} %bitcast.75), channel_id=2, replica_groups=mesh['z'=8,'x'=4,'y'=8,'core'=2] {'y','core'}, dimensions={0}, use_global_device_ids=true | all-gather | bytes 34816 | tf_op jit(solution)/shard_map/all_gather | solution.py:225
  51.9 1.8 %multiply_reduce_fusion = f32[8,128]{1,0:T(8,128)S(1)} fusion(bf16[8,128,768]{2,1,0:T(8,128)(2,1)} %cents_ref.1), kind=kLoop, calls=%fused_computation.4 | loop fusion | flops 2358272 | bytes 1576960 | tf_op jit(solution)/shard_map/reduce_sum | solution.py:229
  54.0 0.5 slice.61
  54.5 1.2 fusion.20
  56.4 20.0 %all-to-all-done = f16[32,8,3968]{2,1,0:T(8,128)(2,1)S(1)} async-done(((f16[32,8,3968]{2,1,0:T(8,128)(2,1)}), f16[32,8,3968]{2,1,0:T(8,128)(2,1)S(1)}, u32[]{:S(2)}, u32[]{:S(2)}) %all-to-all-start) | async-done | bytes 2031648 | tf_op jit(solution)/shard_map/all_to_all | solution.py:224
  76.4 0.7 add_add_fusion
  77.4 1.0 exponential_reduce_fusion
  78.5 1.4 convolution_select_fusion
  80.4 0.8 convolution_add_fusion
  81.5 4.5 %collective-permute-start = (f32[8,8,3968]{2,1,0:T(8,128)S(1)}, f32[8,8,3968]{2,1,0:T(8,128)S(1)}, u32[]{:S(2)}, u32[]{:S(2)}) collective-permute-start(f32[8,8,3968]{2,1,0:T(8,128)S(1)} %get-tuple-element.9), channel_id=1, source_target_pairs={{0,1},{1,0},{2,3},{3,2},{4,5},{5,4},{6,7},{7,6},{8,9},{9,8},{10,11... | collective-permute-start | bytes 3047432 | tf_op jit(solution)/shard_map/ppermute | solution.py:254
  86.0 2.2 %collective-permute-done.got_ref = f32[8,8,3968]{2,1,0:T(8,128)S(1)} collective-permute-done((f32[8,8,3968]{2,1,0:T(8,128)S(1)}, f32[8,8,3968]{2,1,0:T(8,128)S(1)}, u32[]{:S(2)}, u32[]{:S(2)}) %collective-permute-start) | collective-permute-done | bytes 1015840 | tf_op jit(solution)/shard_map/ppermute | solution.py:254
  88.4 0.9 convert_element_type.74
  89.3 6.8 %all-to-all-start.1 = ((f16[8,8,3968]{2,1,0:T(8,128)(2,1)}), f16[8,8,3968]{2,1,0:T(8,128)(2,1)S(1)}, u32[]{:S(2)}, u32[]{:S(2)}) async-start(f16[8,8,3968]{2,1,0:T(8,128)(2,1)} %convert_element_type.74), calls=%async_computation.1 | async-start | bytes 1015808 | tf_op jit(solution)/shard_map/all_to_all | solution.py:256
  96.1 0.7 constant_dynamic-slice_fusion.2.coarse_ref
  97.1 1.2 slice.66
  99.4 9.9 %shard_map.78 = f32[16,1,512]{2,1,0:T(1,128)} custom-call(s32[16]{0:T(128)} %broadcast_add_fusion.1.pick_ref, bf16[8,128,768]{2,1,0:T(8,128)(2,1)} %cents_ref.1, f32[8,128,1]{2,1,0:T(8,128)} %copy-done.6, bf16[16,512,768]{2,1,0:T(8,128)(2,1)} %bitcast.70), custom_call_target="tpu_custom_call" | custom-call | flops 1610612736 | bytes 12582912 | tf_op jit(solution)/shard_map/pallas_call | solution.py:101
  109.3 0.8 copy.37
  111.2 2.5 %all-to-all-done.1 = f16[8,8,3968]{2,1,0:T(8,128)(2,1)S(1)} async-done(((f16[8,8,3968]{2,1,0:T(8,128)(2,1)}), f16[8,8,3968]{2,1,0:T(8,128)(2,1)S(1)}, u32[]{:S(2)}, u32[]{:S(2)}) %all-to-all-start.1) | async-done | bytes 507936 | tf_op jit(solution)/shard_map/all_to_all | solution.py:256
  113.8 0.8 shard_map.79
  114.6 18.3 %all-gather.4 = f32[16,28,512]{2,1,0:T(8,128)S(1)} all-gather(f32[1,28,512]{2,1,0:T(8,128)S(1)} %bitcast.67), channel_id=4, replica_groups=mesh['z'=8,'x'=4,'y'=8,'core'=2] {'y','core'}, dimensions={0}, use_global_device_ids=true | all-gather | bytes 974848 | tf_op jit(solution)/shard_map/all_gather | solution.py:262
  133.0 0.6 add_multiply_fusion
  133.6 0.8 maximum_bitcast_fusion
  (35 shorter events, 3.7 us)
Async XLA Ops:
  7.2 92.3 %all-gather.7.cloned.1.call-start = ((), (), s32[]{:S(2)}) async-start(), calls=%async_computation.2 | async-start | bytes 13369344 | tf_op jit(solution)/shard_map/all_gather | solution.py:220
  7.9 1.1 copy-start.1
  9.0 0.7 copy-start.3
  9.7 0.7 copy-start.5
  12.0 1.9 %copy-start = (f32[256,3968]{1,0:T(8,128)}, f32[256,3968]{1,0:T(8,128)S(1)}, u32[]{:S(2)}) copy-start(f32[256,3968]{1,0:T(8,128)S(1)} %shard_map.76) | copy-start | bytes 12189700
  15.4 17.8 %copy-start.4 = (s32[512]{0:T(512)S(1)}, s32[512]{0:T(512)}, u32[]{:S(2)}) copy-start(s32[512]{0:T(512)} %param.6) | copy-start | bytes 6148
  15.4 61.0 %all-to-all-start = ((f16[32,8,3968]{2,1,0:T(8,128)(2,1)}), f16[32,8,3968]{2,1,0:T(8,128)(2,1)S(1)}, u32[]{:S(2)}, u32[]{:S(2)}) async-start(f16[32,8,3968]{2,1,0:T(8,128)(2,1)} %convert_bitcast_fusion), calls=%async_computation | async-start | bytes 4063232 | tf_op jit(solution)/shard_map/all_to_all | solution.py:224
  54.0 26.4 %copy-start.6 = (f32[8,128,1]{2,1,0:T(8,128)}, f32[8,128,1]{2,1,0:T(8,128)S(1)}, u32[]{:S(2)}) copy-start(f32[8,128,1]{2,1,0:T(8,128)S(1)} %copy.22.square_ref) | copy-start | bytes 12292
  81.5 6.8 %collective-permute-start = (f32[8,8,3968]{2,1,0:T(8,128)S(1)}, f32[8,8,3968]{2,1,0:T(8,128)S(1)}, u32[]{:S(2)}, u32[]{:S(2)}) collective-permute-start(f32[8,8,3968]{2,1,0:T(8,128)S(1)} %get-tuple-element.9), channel_id=1, source_target_pairs={{0,1},{1,0},{2,3},{3,2},{4,5},{5,4},{6,7},{7,6},{8,9},{9,8},{10,11... | collective-permute-start | bytes 3047432 | tf_op jit(solution)/shard_map/ppermute | solution.py:254
  88.4 8.4 %copy-start.2 = (bf16[512,768]{1,0:T(8,128)(2,1)S(1)}, bf16[512,768]{1,0:T(8,128)(2,1)}, u32[]{:S(2)}) copy-start(bf16[512,768]{1,0:T(8,128)(2,1)} %rows_ref.1) | copy-start | bytes 2359300
  89.3 24.4 %all-to-all-start.1 = ((f16[8,8,3968]{2,1,0:T(8,128)(2,1)}), f16[8,8,3968]{2,1,0:T(8,128)(2,1)S(1)}, u32[]{:S(2)}, u32[]{:S(2)}) async-start(f16[8,8,3968]{2,1,0:T(8,128)(2,1)} %convert_element_type.74), calls=%async_computation.1 | async-start | bytes 1015808 | tf_op jit(solution)/shard_map/all_to_all | solution.py:256
Sparse Core Ops, SparseCore 0:
  10.1 84.0 all-gather.6

commit v7 on v6

--- a/solution.py
+++ b/solution.py
@@ -15,13 +15,13 @@
 LARGE = 56 * 2**20
 
 
-def message_kernel(share, owned, coarse_ref, fine_ref, rows_ref, out_ref):
+def message_kernel(share, owned, fine_ref, rows_ref, out_ref):
     count, width = rows_ref.shape
     per = 128
     lines = out_ref.shape[0]
     slots = 8
-    coarse = coarse_ref[...]
-    local = fine_ref[...] - coarse * per
+    coarse = fine_ref[...] // per
+    local = fine_ref[...] % per
     owner = coarse // owned
 
     owners = lax.broadcasted_iota(jnp.int32, (16, count), 0)
@@ -62,19 +62,19 @@
     out_ref[:, (share + 1) * width :] = notes
 
 
-def message_of(coarse_ids, fine_ids, rows, planes, share, owned):
+def message_of(fine_ids, rows, planes, share, owned):
     width = rows.shape[1]
     shape = (planes * 8, (share + 1) * width + 128)
     return pl.pallas_call(
         functools.partial(message_kernel, share, owned),
-        in_specs=[pl.BlockSpec(memory_space=pltpu.VMEM)] * 3,
+        in_specs=[pl.BlockSpec(memory_space=pltpu.VMEM)] * 2,
         out_specs=pl.BlockSpec(memory_space=pltpu.VMEM),
         out_shape=jax.ShapeDtypeStruct(shape, jnp.float32),
         compiler_params=pltpu.CompilerParams(vmem_limit_bytes=SMALL),
         cost_estimate=pl.CostEstimate(
             flops=2 * shape[0] * shape[1] * rows.shape[0], bytes_accessed=16 * rows.size, transcendentals=0
         ),
-    )(coarse_ids[None, :], fine_ids[None, :], rows)
+    )(fine_ids[None, :], rows)
 
 
 def gaps_kernel(pick_ref, cents_ref, square_ref, rows_ref, out_ref, held, sems):
@@ -219,9 +219,9 @@
 
     rows = lax.all_gather(embeds, CENT, axis=0, tiled=False)
 
-    message = message_of(coarse_ids, fine_ids, embeds, planes, share, blk)
-    heard = message.astype(jnp.float16).reshape(planes, slots, -1)
-    heard = lax.all_to_all(heard, DP, split_axis=0, concat_axis=0, tiled=True)
+    message = message_of(fine_ids, embeds, planes, share, blk)
+    message = message.astype(jnp.float16).reshape(planes, slots, -1)
+    heard = lax.all_to_all(message, DP, split_axis=0, concat_axis=0, tiled=True)
     sent = lax.all_gather(after(coarse_ids, message), CENT, axis=0, tiled=False)
 
     near = sent - me * blk

time: 142 us -> 140 us (0.986)
  local copies, waits for them, and re-layouts: 10.7 us -> 8.17 us
    unnamed x16 -> x12, local copies, waits for them, and re-layouts: 5.19 us -> 2.61 us
where the time goes in v7:
time: 140 us; the launch traced here: 139 us
  blocking collectives  36.8 us (26%)
  starting transfers between devices  25.5 us (18%)
  waiting for transfers between devices  25.3 us (18%)
  between operations  17.6 us (13%)
  Pallas kernels  12.5 us (9%)
  other arithmetic  10.5 us (8%)
  local copies, waits for them, and re-layouts  8.17 us (6%)
  matrix products  2.65 us (2%)
    all_to_all x1, waiting for transfers between devices, body(): heard = lax.all_to_all(message, DP, split_axis=0, concat_axis=0, tiled=True)  20 us
    all_gather x1, blocking collectives, body(): sent = lax.all_gather(after(coarse_ids, message), CENT, axis=0, tiled=False)  18.5 us
    all_gather x1, blocking collectives, body(): news = lax.all_gather(news, CENT, axis=0, tiled=False)  18.3 us
    all_to_all x1, starting transfers between devices, body(): heard = lax.all_to_all(message, DP, split_axis=0, concat_axis=0, tiled=True)  13.8 us
    pallas_call x1, Pallas kernels, nearest(): pl.pallas_call(gaps_kernel, in_specs=[pl.BlockSpec(memory_space=pltpu.SME...  9.88 us
    all_to_all x1, starting transfers between devices, body(): arrived = lax.all_to_all(both, 'y', split_axis=0, concat_axis=0, tiled=True)  7.1 us
    ppermute x1, starting transfers between devices, body(): got = lax.ppermute(given, 'core', [(0, 1), (1, 0)])  4.51 us
    slice x5, local copies, waits for them, and re-layouts, after(): earlier[(0,) * earlier.ndim].astype(jnp.float32) * 0.0  3.95 us
  transfers between devices with their start and end apart: 4, of which 3 were waited for; matrix products, arithmetic and copies ran while one was open for 13% of the time, Pallas kernels for 8%

profile of v7, /device:TPU:1, one launch (start us, length us, event | category | flops | bytes accessed | tf_op | source)
XLA Modules:
  0.0 139.0 jit_solution(16532925376158610789)
XLA Ops:
  7.2 0.7 all-gather.7.cloned.1.call-update
  7.9 1.1 copy-done
  9.0 0.7 copy-done.2
  9.7 1.6 %shard_map.76 = f32[256,3968]{1,0:T(8,128)S(1)} custom-call(s32[1,512]{1,0:T(1,128)S(1)} %bitcast.67, bf16[512,768]{1,0:T(8,128)(2,1)S(1)} %copy-done), custom_call_target="tpu_custom_call" | custom-call | flops 1040187392 | bytes 6291456 | tf_op jit(solution)/shard_map/pallas_call | solution.py:68
  11.3 1.5 %convert_bitcast_fusion = f16[32,8,3968]{2,1,0:T(8,128)(2,1)} fusion(f32[256,3968]{1,0:T(8,128)S(1)} %shard_map.76), kind=kLoop, calls=%fused_computation.6 | loop fusion | flops 1015808 | bytes 6094848 | tf_op jit(solution)/shard_map/reshape | solution.py:223
  12.8 13.8 %all-to-all-start = ((f16[32,8,3968]{2,1,0:T(8,128)(2,1)}), f16[32,8,3968]{2,1,0:T(8,128)(2,1)S(1)}, u32[]{:S(2)}, u32[]{:S(2)}) async-start(f16[32,8,3968]{2,1,0:T(8,128)(2,1)} %convert_bitcast_fusion), calls=%async_computation | async-start | bytes 4063232 | tf_op jit(solution)/shard_map/all_to_all | solution.py:224
  26.7 1.2 slice.60
  27.9 0.9 convert_bitcast_fusion.1
  28.8 0.5 slice.62
  30.1 18.5 %all-gather.3 = s32[16,1,512]{2,1,0:T(1,128)S(1)} all-gather(s32[1,1,512]{2,1,0:T(1,128)S(1)} %bitcast.73), channel_id=2, replica_groups=mesh['z'=8,'x'=4,'y'=8,'core'=2] {'y','core'}, dimensions={0}, use_global_device_ids=true | all-gather | bytes 34816 | tf_op jit(solution)/shard_map/all_gather | solution.py:225
  48.7 1.8 %multiply_reduce_fusion = f32[8,128]{1,0:T(8,128)S(1)} fusion(bf16[8,128,768]{2,1,0:T(8,128)(2,1)} %cents_ref.1), kind=kLoop, calls=%fused_computation.4 | loop fusion | flops 2358272 | bytes 1576960 | tf_op jit(solution)/shard_map/reduce_sum | solution.py:229
  50.8 0.6 slice.61
  52.0 1.2 fusion.20
  53.9 20.0 %all-to-all-done = f16[32,8,3968]{2,1,0:T(8,128)(2,1)S(1)} async-done(((f16[32,8,3968]{2,1,0:T(8,128)(2,1)}), f16[32,8,3968]{2,1,0:T(8,128)(2,1)S(1)}, u32[]{:S(2)}, u32[]{:S(2)}) %all-to-all-start) | async-done | bytes 2031648 | tf_op jit(solution)/shard_map/all_to_all | solution.py:224
  73.8 0.7 add_add_fusion
  74.8 1.0 exponential_reduce_fusion
  76.0 1.4 %convolution_select_fusion = f32[128,128]{1,0:T(8,128)S(1)} fusion(f32[256]{0:T(256)S(1)} %eq.42, f32[]{:T(128)} %get-tuple-element.8, pred[128]{0:T(512)(128)(4,1)S(1)} %iota_compare_fusion.3, f16[32,8,3968]{2,1,0:T(8,128)(2,1)S(1)} %all-to-all-done, f32[]{:T(128)} %bitcast.8, f32[]{:T(128)} %bitcast.7, f32[]{:T(128)} %bitcast.6, f32[]{:T(128)} %bitcast.4), kind=kOutput, calls=%fused_computation.10 | convolution fusion | flops 8634368 | bytes 132628 | tf_op jit(solution)/shard_map/dot_general | solution.py:248
  77.9 0.8 convolution_add_fusion
  78.9 4.5 %collective-permute-start = (f32[8,8,3968]{2,1,0:T(8,128)S(1)}, f32[8,8,3968]{2,1,0:T(8,128)S(1)}, u32[]{:S(2)}, u32[]{:S(2)}) collective-permute-start(f32[8,8,3968]{2,1,0:T(8,128)S(1)} %get-tuple-element.9), channel_id=1, source_target_pairs={{0,1},{1,0},{2,3},{3,2},{4,5},{5,4},{6,7},{7,6},{8,9},{9,8},{10,11... | collective-permute-start | bytes 3047432 | tf_op jit(solution)/shard_map/ppermute | solution.py:254
  83.5 2.2 %collective-permute-done.got_ref = f32[8,8,3968]{2,1,0:T(8,128)S(1)} collective-permute-done((f32[8,8,3968]{2,1,0:T(8,128)S(1)}, f32[8,8,3968]{2,1,0:T(8,128)S(1)}, u32[]{:S(2)}, u32[]{:S(2)}) %collective-permute-start) | collective-permute-done | bytes 1015840 | tf_op jit(solution)/shard_map/ppermute | solution.py:254
  85.9 0.9 convert_element_type.79
  86.7 7.1 %all-to-all-start.1 = ((f16[8,8,3968]{2,1,0:T(8,128)(2,1)}), f16[8,8,3968]{2,1,0:T(8,128)(2,1)S(1)}, u32[]{:S(2)}, u32[]{:S(2)}) async-start(f16[8,8,3968]{2,1,0:T(8,128)(2,1)} %convert_element_type.79), calls=%async_computation.1 | async-start | bytes 1015808 | tf_op jit(solution)/shard_map/all_to_all | solution.py:256
  93.8 0.7 constant_dynamic-slice_fusion.2.coarse_ref
  94.8 1.2 slice.66
  96.7 0.5 broadcast_add_fusion.1.pick_ref
  97.2 9.9 %shard_map.78 = f32[16,1,512]{2,1,0:T(1,128)} custom-call(s32[16]{0:T(128)} %broadcast_add_fusion.1.pick_ref, bf16[8,128,768]{2,1,0:T(8,128)(2,1)} %cents_ref.1, f32[8,128,1]{2,1,0:T(8,128)} %copy-done.3, bf16[16,512,768]{2,1,0:T(8,128)(2,1)} %bitcast.68), custom_call_target="tpu_custom_call" | custom-call | flops 1610612736 | bytes 12582912 | tf_op jit(solution)/shard_map/pallas_call | solution.py:101
  107.1 0.8 copy.31
  109.0 2.5 %all-to-all-done.1 = f16[8,8,3968]{2,1,0:T(8,128)(2,1)S(1)} async-done(((f16[8,8,3968]{2,1,0:T(8,128)(2,1)}), f16[8,8,3968]{2,1,0:T(8,128)(2,1)S(1)}, u32[]{:S(2)}, u32[]{:S(2)}) %all-to-all-start.1) | async-done | bytes 507936 | tf_op jit(solution)/shard_map/all_to_all | solution.py:256
  111.5 0.8 shard_map.79
  112.4 18.3 %all-gather.4 = f32[16,28,512]{2,1,0:T(8,128)S(1)} all-gather(f32[1,28,512]{2,1,0:T(8,128)S(1)} %bitcast.66), channel_id=4, replica_groups=mesh['z'=8,'x'=4,'y'=8,'core'=2] {'y','core'}, dimensions={0}, use_global_device_ids=true | all-gather | bytes 974848 | tf_op jit(solution)/shard_map/all_gather | solution.py:262
  130.7 0.6 add_multiply_fusion
  131.3 0.8 maximum_bitcast_fusion
  (31 shorter events, 2.7 us)
Async XLA Ops:
  7.2 90.0 %all-gather.7.cloned.1.call-start = ((), (), s32[]{:S(2)}) async-start(), calls=%async_computation.2 | async-start | bytes 13369344 | tf_op jit(solution)/shard_map/all_gather | solution.py:220
  7.9 1.1 copy-start
  9.0 0.7 copy-start.2
  12.8 17.2 %copy-start.4 = (s32[512]{0:T(512)S(1)}, s32[512]{0:T(512)}, u32[]{:S(2)}) copy-start(s32[512]{0:T(512)} %param.6) | copy-start | bytes 6148
  12.8 61.0 %all-to-all-start = ((f16[32,8,3968]{2,1,0:T(8,128)(2,1)}), f16[32,8,3968]{2,1,0:T(8,128)(2,1)S(1)}, u32[]{:S(2)}, u32[]{:S(2)}) async-start(f16[32,8,3968]{2,1,0:T(8,128)(2,1)} %convert_bitcast_fusion), calls=%async_computation | async-start | bytes 4063232 | tf_op jit(solution)/shard_map/all_to_all | solution.py:224
  50.8 27.1 %copy-start.3 = (f32[8,128,1]{2,1,0:T(8,128)}, f32[8,128,1]{2,1,0:T(8,128)S(1)}, u32[]{:S(2)}) copy-start(f32[8,128,1]{2,1,0:T(8,128)S(1)} %copy.16.square_ref) | copy-start | bytes 12292
  78.9 6.7 %collective-permute-start = (f32[8,8,3968]{2,1,0:T(8,128)S(1)}, f32[8,8,3968]{2,1,0:T(8,128)S(1)}, u32[]{:S(2)}, u32[]{:S(2)}) collective-permute-start(f32[8,8,3968]{2,1,0:T(8,128)S(1)} %get-tuple-element.9), channel_id=1, source_target_pairs={{0,1},{1,0},{2,3},{3,2},{4,5},{5,4},{6,7},{7,6},{8,9},{9,8},{10,11... | collective-permute-start | bytes 3047432 | tf_op jit(solution)/shard_map/ppermute | solution.py:254
  85.9 8.7 %copy-start.1 = (bf16[512,768]{1,0:T(8,128)(2,1)S(1)}, bf16[512,768]{1,0:T(8,128)(2,1)}, u32[]{:S(2)}) copy-start(bf16[512,768]{1,0:T(8,128)(2,1)} %rows_ref.1) | copy-start | bytes 2359300
  86.7 24.7 %all-to-all-start.1 = ((f16[8,8,3968]{2,1,0:T(8,128)(2,1)}), f16[8,8,3968]{2,1,0:T(8,128)(2,1)S(1)}, u32[]{:S(2)}, u32[]{:S(2)}) async-start(f16[8,8,3968]{2,1,0:T(8,128)(2,1)} %convert_element_type.79), calls=%async_computation.1 | async-start | bytes 1015808 | tf_op jit(solution)/shard_map/all_to_all | solution.py:256
Sparse Core Ops, SparseCore 0:
  10.1 84.0 all-gather.6
